TPU v7x, 768 devices: a whole 4x8x12 slice. The times are simulated.
768 devices in a mesh: dp: 16 (over y, core), fsdp: 48 (over z, x).
Axes of the slice: x: 4, y: 8, z: 12, core: 2. Of those that a mesh axis runs over, the one named last changes fastest.
Arguments:
- x_slots: bfloat16 [48, 3072, 4608], P('fsdp', None, 'dp'), may hold values from -6 to 6
- gain: bfloat16 [4608], P('fsdp'), may hold values from 0.099609375 to 1.8984375
- adapter: bfloat16 [4608, 256], P('fsdp'), may hold values from -0.09375 to 0.09375
- readout: bfloat16 [48, 3072, 256], P('fsdp'), may hold values from -0.1875 to 0.1875
- drift: float32 [48, 3072], P('fsdp'), may hold values from -0.6 to 0.6
- ref_gap: float32 [48, 3072], P('fsdp'), may hold values from -2 to 2
- rewards: float32 [48, 48], P('fsdp'), may hold values from -4 to 4
- groups: int32 [48, 48], P('fsdp'), may hold values from 0 to 11, never falling along the last dimension, each value on 1 to 8 neighbouring positions
- lengths: int32 [48, 48], P('fsdp'), may hold values from 1 to 64, as said below
- dest: int32 [48, 48], P('fsdp'), may hold values from 0 to 15, as said below
Outputs:
- grad_adapter: float32 [4608, 256], P('fsdp')
- grad_gain: float32 [4608], P('fsdp')
Inputs may be any that keep to these rules, and one draw needn't show every extreme that they name: `dest`: each learner rank receives exactly 3 rollouts of every column. `lengths`: in every column, all rollouts of some learner rank have 64 tokens, so that some rank holds exactly 192 live tokens. `groups`: within a column group numbers never fall; a group has 1 to 8 rollouts.
All inputs are finite; a program needn't handle non-finite values.
Results may differ from a plain program's by a relative error of at most 0.0045.
Values may be sent and summed in bfloat16 or wider, within the bound.
A program may use at most 64 MiB of HBM per device.

v0:
```python
import math

import jax
import jax.numpy as jnp
from jax import lax
from jax.sharding import PartitionSpec as P

kl_coef = 0.1
norm_eps = 1e-06
upper_log = math.log(1.2)
lower_log = math.log(0.8)


def advantages(rewards, groups):
    same_group = (groups[..., :, None] == groups[..., None, :]).astype(rewards.dtype)
    members = jnp.sum(same_group, -1)
    group_mean = jnp.sum(same_group * rewards[..., None, :], -1) / members
    spread = (
        jnp.sum(same_group * (rewards[..., None, :] - group_mean[..., :, None]) ** 2, -1) / members
    )
    return (rewards - group_mean) / jnp.sqrt(jnp.maximum(spread, 0.25))


def latent_grad(latent, readout_rows, drift_rows, gap_rows, adv_rows, weight):
    readout_f = readout_rows.astype(jnp.float32)
    shift_value = jnp.sum(latent * readout_f, -1)
    logratio = drift_rows + shift_value
    ratio_value = jnp.exp(logratio)
    upper = jnp.asarray(upper_log, drift_rows.dtype)
    lower = jnp.asarray(lower_log, drift_rows.dtype)
    keep_mask = jnp.where(adv_rows >= 0, drift_rows <= upper, drift_rows >= lower).astype(
        drift_rows.dtype
    )
    dshift = weight * (
        -adv_rows * ratio_value * keep_mask + kl_coef * (1.0 - jnp.exp(gap_rows - logratio))
    )
    return (dshift[:, None] * readout_f).astype(jnp.bfloat16)


def per_device(x_slots, gain, adapter, readout, drift, ref_gap, rewards, groups, lengths, dest):
    rank_count = lax.axis_size("dp")
    my_rank = lax.axis_index("dp")
    roll_lengths = lengths[0]
    targets = dest[0]
    roll_count = roll_lengths.shape[0]
    slot_span = x_slots.shape[1] // roll_count
    tok_rows = roll_count // rank_count * slot_span
    roll_order = jnp.arange(roll_count)
    same_rank = targets[None, :] == targets[:, None]
    earlier = same_rank & (roll_order[None, :] < roll_order[:, None])
    offsets = jnp.sum(jnp.where(earlier, roll_lengths[None, :], 0), axis=1)
    row_places = jnp.arange(tok_rows)
    rank_ids = jnp.arange(rank_count)
    inside = (
        (targets[None, None, :] == rank_ids[:, None, None])
        & (row_places[None, :, None] >= offsets[None, None, :])
        & (row_places[None, :, None] < (offsets + roll_lengths)[None, None, :])
    )
    hit_table = inside.astype(jnp.int32)
    row_valid = jnp.sum(hit_table, axis=2) > 0
    source_row = (
        jnp.sum(hit_table * (roll_order * slot_span - offsets)[None, None, :], axis=2)
        + row_places[None, :]
    )
    source_row = jnp.where(row_valid, source_row, 0)
    local_rows = x_slots[0]
    outgoing = jnp.where(
        row_valid.reshape(-1)[:, None],
        local_rows[source_row.reshape(-1)],
        jnp.zeros((), local_rows.dtype),
    )
    arrived = lax.all_to_all(outgoing, "dp", split_axis=0, concat_axis=1, tiled=True)
    my_rows = lax.dynamic_index_in_dim(source_row, my_rank, 0, keepdims=False)
    my_valid = lax.dynamic_index_in_dim(row_valid, my_rank, 0, keepdims=False)
    my_hits = lax.dynamic_index_in_dim(hit_table, my_rank, 0, keepdims=False).astype(jnp.float32)
    advantage = advantages(rewards[0], groups[0])
    adv_rows = jnp.sum(my_hits * advantage[None, :], axis=1)
    rank_tokens = jnp.sum(jnp.where(targets == my_rank, roll_lengths, 0)).astype(jnp.float32)
    weight = jnp.where(my_valid, 1.0 / rank_tokens, jnp.zeros((), jnp.float32))
    readout_rows = readout[0][my_rows]
    drift_rows = drift[0][my_rows]
    gap_rows = ref_gap[0][my_rows]
    x_float = arrived.astype(jnp.float32)
    normed = x_float * lax.rsqrt(jnp.mean(x_float * x_float, -1, keepdims=True) + norm_eps)
    weight_piece = lax.all_gather(adapter, "fsdp", axis=0, tiled=True)
    gain_piece = lax.all_gather(gain, "fsdp", axis=0, tiled=True)
    z_block = (normed * gain_piece.astype(jnp.float32)).astype(jnp.bfloat16)
    z_whole = z_block
    latent_sum = jnp.dot(z_block, weight_piece, preferred_element_type=jnp.float32)
    dlatent = latent_grad(latent_sum, readout_rows, drift_rows, gap_rows, adv_rows, weight)
    z_block = z_whole
    shard_sum = lax.psum_scatter(
        lax.dot_general(
            z_block, dlatent, (((0,), (0,)), ((), ())), preferred_element_type=jnp.float32
        ),
        "fsdp",
        scatter_dimension=0,
        tiled=True,
    )
    grad_adapter = lax.psum(shard_sum, "dp")
    grad_gain = jnp.sum(adapter.astype(jnp.float32) * grad_adapter, 1) / gain.astype(jnp.float32)
    return (grad_adapter, grad_gain)


def solution(mesh):
    in_specs = (
        P("fsdp", None, "dp"),
        P("fsdp"),
        P("fsdp", None),
        P("fsdp", None, None),
        P("fsdp", None),
        P("fsdp", None),
        P("fsdp", None),
        P("fsdp", None),
        P("fsdp", None),
        P("fsdp", None),
    )
    out_specs = (P("fsdp", None), P("fsdp"))
    return jax.shard_map(
        per_device, mesh=mesh, in_specs=in_specs, out_specs=out_specs, check_vma=False
    )
```

profile of v0, /device:TPU:1, one launch (start us, length us, event | category | flops | bytes accessed | tf_op | source)
XLA Modules:
  0.0 839.7 jit_solution(14546500334320252644)
XLA Ops:
  7.2 0.0 copy-start
  7.2 0.0 all-gather.2.cloned.1.call-start
  7.2 0.7 all-gather.2.cloned.1.call-update
  7.9 0.7 iota_compare_fusion.3
  8.6 0.9 select_reduce_fusion.1
  9.5 1.3 fusion.15
  10.8 0.1 iota_compare_fusion
  10.9 0.3 select_reduce_fusion
  11.3 0.1 select_n.79
  11.4 4.0 copy.18
  15.4 14.7 %gather_fusion = bf16[3072,288]{1,0:T(8,128)(2,1)} fusion(bf16[3072,288]{1,0:T(8,128)(2,1)} %bitcast.36, s32[3072]{0:T(1024)S(1)} %broadcast_clamp_fusion), kind=kCustom, calls=%fused_computation | custom fusion | bytes 3551232 | tf_op jit(solution)/shard_map/gather | solution.py:69
  30.1 2.9 broadcast_select_fusion
  33.0 14.8 %all-to-all-start = ((bf16[16,192,288]{2,1,0:T(8,128)(2,1)}), bf16[16,192,288]{2,1,0:T(8,128)(2,1)}, u32[]{:S(2)}, u32[]{:S(2)}) async-start(bf16[16,192,288]{2,1,0:T(8,128)(2,1)} %broadcast_select_fusion), calls=%async_computation | async-start | bytes 4718592 | tf_op jit(solution)/shard_map/all_to_all | solution.py:72
  47.9 0.0 copy-start.6
  47.9 0.0 reduce-scatter.2.cloned.1.call-start
  48.0 1.3 dynamic-slice
  49.9 0.0 copy-done.7
  49.9 0.2 dynamic-update-slice
  50.2 176.3 %all-reduce = bf16[4608]{0:T(1024)(128)(2,1)S(1)} all-reduce(bf16[4608]{0:T(1024)(128)(2,1)S(1)} %dynamic-update-slice), channel_id=1, replica_groups=mesh['dp'=16,'fsdp'=48] {'fsdp'}, use_global_device_ids=true, to_apply=%add | all-reduce | flops 4608 | bytes 18432
  227.2 0.0 copy-done
  227.2 1.0 gather_fusion.2
  228.2 0.0 copy-done.1
  228.2 1.4 gather_fusion.1
  229.7 0.0 copy-done.2
  229.7 1.4 gather_fusion.3
  231.2 0.0 copy-done.5
  231.2 0.0 copy-done.6
  231.2 0.2 fusion.10
  231.4 0.2 fusion.11
  231.6 0.2 fusion.2
  231.8 0.1 fusion.8
  231.9 0.0 all-to-all-done
  231.9 2.1 convert_bitcast_fusion
  234.0 4.9 copy.19
  238.9 5.7 reshape.259
  244.6 2.3 fusion
  246.8 0.0 all-gather.2.cloned.1.call-done
  246.9 3.7 fusion.1
  250.6 0.1 copy-done.3
  250.6 3.1 fusion.5
  253.7 0.0 reduce-scatter.2.cloned.1.call-update
  253.7 0.0 all-reduce.3.cloned.1.call-start
  253.7 453.0 %reduce-scatter.2.cloned.1.call-done = f32[96,256]{1,0:T(8,128)} async-done(((f32[4608,256]{1,0:T(8,128)}), f32[96,256]{1,0:T(8,128)}) %reduce-scatter.2.cloned.1.call-update) | async-done | bytes 98320 | tf_op jit(solution)/shard_map/reduce_scatter | solution.py:92
  706.7 0.0 all-reduce.3.cloned.1.call-update
  706.7 123.4 %all-reduce.3.cloned.1.call-done = f32[96,256]{1,0:T(8,128)} async-done(((f32[96,256]{1,0:T(8,128)}), f32[96,256]{1,0:T(8,128)}) %all-reduce.3.cloned.1.call-update) | async-done | bytes 98320 | tf_op jit(solution)/shard_map/psum | solution.py:100
  830.1 1.0 multiply_reduce_fusion
  831.1 0.5 convert_divide_fusion
  831.6 1.5 copy.22
  (19 shorter events, 0.1 us)
Async XLA Ops:
  7.2 220.0 %copy-start = (bf16[1,3072,256]{2,1,0:T(8,128)(2,1)S(1)}, bf16[1,3072,256]{2,1,0:T(8,128)(2,1)}, u32[]{:S(2)}) copy-start(bf16[1,3072,256]{2,1,0:T(8,128)(2,1)} %param.13) | copy-start | bytes 4718596
  7.2 239.7 %all-gather.2.cloned.1.call-start = ((), (), s32[]{:S(2)}) async-start(), calls=%async_computation.2 | async-start | bytes 2408448 | tf_op jit(solution)/shard_map/all_gather | solution.py:85
  33.0 16.9 %copy-start.7 = (bf16[96]{0:T(256)(128)(2,1)S(1)}, bf16[96]{0:T(256)(128)(2,1)}, u32[]{:S(2)}) copy-start(bf16[96]{0:T(256)(128)(2,1)} %param.11) | copy-start | bytes 580
  33.0 195.2 %copy-start.1 = (f32[1,3072]{1,0:T(1,128)S(1)}, f32[1,3072]{1,0:T(1,128)}, u32[]{:S(2)}) copy-start(f32[1,3072]{1,0:T(1,128)} %param.14) | copy-start | bytes 36868
  33.0 196.6 %copy-start.2 = (f32[1,3072]{1,0:T(1,128)S(1)}, f32[1,3072]{1,0:T(1,128)}, u32[]{:S(2)}) copy-start(f32[1,3072]{1,0:T(1,128)} %param.15) | copy-start | bytes 36868
  33.0 198.8 %all-to-all-start = ((bf16[16,192,288]{2,1,0:T(8,128)(2,1)}), bf16[16,192,288]{2,1,0:T(8,128)(2,1)}, u32[]{:S(2)}, u32[]{:S(2)}) async-start(bf16[16,192,288]{2,1,0:T(8,128)(2,1)} %broadcast_select_fusion), calls=%async_computation | async-start | bytes 4718592 | tf_op jit(solution)/shard_map/all_to_all | solution.py:72
  47.9 183.3 %copy-start.5 = (s32[1,48]{1,0:T(1,128)S(1)}, s32[1,48]{1,0:T(1,128)}, u32[]{:S(2)}) copy-start(s32[1,48]{1,0:T(1,128)} %param.17) | copy-start | bytes 580
  47.9 183.3 %copy-start.6 = (f32[1,48]{1,0:T(1,128)S(1)}, f32[1,48]{1,0:T(1,128)}, u32[]{:S(2)}) copy-start(f32[1,48]{1,0:T(1,128)} %param.16) | copy-start | bytes 580
  47.9 658.8 %reduce-scatter.2.cloned.1.call-start = ((), (), s32[]{:S(2)}) async-start(), calls=%async_computation.3 | async-start | bytes 4816896 | tf_op jit(solution)/shard_map/reduce_scatter | solution.py:92
  246.9 3.8 copy-start.3
  253.7 576.4 %copy-start.4 = (bf16[96,256]{1,0:T(8,128)(2,1)S(1)}, bf16[96,256]{1,0:T(8,128)(2,1)}, u32[]{:S(2)}) copy-start(bf16[96,256]{1,0:T(8,128)(2,1)} %param.12) | copy-start | bytes 147460
  253.7 576.4 %all-reduce.3.cloned.1.call-start = ((), (), s32[]{:S(2)}) async-start(), calls=%async_computation.4 | async-start | bytes 196608 | tf_op jit(solution)/shard_map/psum | solution.py:100
Sparse Core Ops, SparseCore 0:
  11.6 119.2 all-gather.1
  253.8 452.8 reduce-scatter.1
  709.1 120.9 all-reduce.2
where the time goes:
time: 840 us
  waiting for transfers between devices  577 us (69%)
  blocking collectives  176 us (21%)
  local copies, waits for them, and re-layouts  36.4 us (4%)
  between operations  15.3 us (2%)
  starting transfers between devices  15 us (2%)
  other arithmetic  12.9 us (2%)
    reduce_scatter x1, waiting for transfers between devices, per_device(): lax.psum_scatter(lax.dot_general(z_block, dlatent, (((0,), (0,)), ((), ()...  453 us
    unnamed x1, blocking collectives  176 us
    psum x1, waiting for transfers between devices, per_device(): grad_adapter = lax.psum(shard_sum, 'dp')  123 us
  transfers between devices with their start and end apart: 4, of which 2 were waited for; matrix products, arithmetic and copies ran while one was open for 5% of the time, Pallas kernels for 0%

commit v1 on v0

v1 whole, which is shorter than its diff:
```python
import math

import jax
import jax.numpy as jnp
from jax import lax
from jax.experimental import pallas as pl
from jax.experimental.pallas import tpu as pltpu
from jax.sharding import PartitionSpec as P

WIDTH = 4608
RANK = 256
SLOTS = 3072
LMAX = 64
ROLLS = 48
NP = 16
NZ = 12
NX = 4
FEAT = WIDTH // NP
BLOCK = WIDTH // (NZ * NX)
PER = FEAT // BLOCK
CHUNK = 256
NCH = SLOTS // CHUNK
TILES = 12
kl_coef = 0.1
norm_eps = 1e-06
upper_log = math.log(1.2)
lower_log = math.log(0.8)
F32 = jnp.float32
BF16 = jnp.bfloat16
MESH = pl.DeviceIdType.MESH


def rcopy(src, dst, ssem, rsem, dev):
    return pltpu.make_async_remote_copy(
        src_ref=src, dst_ref=dst, send_sem=ssem, recv_sem=rsem, device_id=dev, device_id_type=MESH
    )


def loop(n, f, start=0):
    def step(i, carry):
        f(i)
        return carry

    lax.fori_loop(start, n, step, jnp.int32(0))


def eye(n, dtype=F32):
    r = lax.broadcasted_iota(jnp.int32, (n, n), 0)
    c = lax.broadcasted_iota(jnp.int32, (n, n), 1)
    return (r == c).astype(F32).astype(dtype)


def contract_last(a, b):
    return lax.dot_general(a, b, (((1,), (1,)), ((), ())), preferred_element_type=F32)


def kernel(
    x_h, gain_h, ad_h, ro_h, drift_h, gap_h, rew_h, grp_h, len_h, dst_h,
    grad_o, ggain_o,
    xv, rv, adv, gainv, driftv, gapv, rewv, grpv, lenv, dstv,
    xT, rT, zT, dT, W, gfull,
    ssp, ssr, rsv, qp, qr, wv,
    AZ, AX, CXs, CX, Sf, CZs, CZ, CD, CF,
    lsem, xsem,
    sAZ, rAZ, sAD, rAD, sAX, rAX,
    sS, rS, sR, rR, sQ, rQ, sW, rW,
    sCX, rCX, sCZ, rCZ, sCD, rCD, sCF, rCF,
):
    p = lax.axis_index("dp")
    c = lax.axis_index("fsdp")
    z = c // NX
    x = c % NX
    kp = jnp.minimum(p, NCH - 1)

    def zdev(z2):
        return (p, z2 * NX + x)

    def xdev(x2):
        return (p, z * NX + x2)

    def ddev(p2):
        return (p2, c)

    def act(x2):
        return lax.rem(x2 + p, 4) != 3

    active = act(x)
    holder = p <= TILES
    owner = p < NCH

    small = [
        (ad_h, adv), (gain_h, gainv), (drift_h, driftv), (gap_h, gapv), (rew_h, rewv),
        (grp_h, grpv), (len_h, lenv), (dst_h, dstv), (ro_h.at[0], rv),
    ]
    loads = [pltpu.make_async_copy(s, d, lsem.at[i]) for i, (s, d) in enumerate(small)]
    XS = SLOTS // 4
    xloads = [
        pltpu.make_async_copy(x_h.at[0, pl.ds(i * XS, XS)], xv.at[pl.ds(i * XS, XS)], xsem.at[i])
        for i in range(4)
    ]
    for d in loads[:2]:
        d.start()
    for d in xloads:
        d.start()
    for d in loads[2:]:
        d.start()

    barrier = pltpu.get_barrier_semaphore()

    def greet(dev):
        pl.semaphore_signal(barrier, inc=1, device_id=dev, device_id_type=MESH)

    loop(NZ, lambda d: greet(zdev(lax.rem(z + d, NZ))), 1)
    loop(NX, lambda d: greet(xdev(lax.rem(x + d, NX))), 1)
    loop(NP, lambda d: greet(ddev(lax.rem(p + d, NP))), 1)
    for d in loads[:2]:
        d.wait()

    for k in range(TILES):
        @pl.when(p == k)
        def _(k=k):
            AZ[z] = adv[16 * (k // 2):16 * (k // 2) + 16, 128 * (k % 2):128 * (k % 2) + 128]

    @pl.when(p == TILES)
    def _():
        row = jnp.concatenate([gainv[...].astype(F32), jnp.ones((1, 128 - BLOCK), F32)], axis=1)
        AZ[z] = jnp.broadcast_to(row, (16, 128)).astype(BF16)

    pl.semaphore_wait(barrier, NZ + NX + NP - 3)

    def az(d):
        return rcopy(AZ.at[z], AZ.at[z], sAZ.at[d], rAZ.at[z], zdev(lax.rem(z + d, NZ)))

    @pl.when(holder)
    def _():
        loop(NZ, lambda d: az(d).start(), 1)

    ident = eye(FEAT, BF16)
    for q in range(4):
        xloads[q].wait()

        def tchunk(i):
            xt = contract_last(ident, xv[pl.ds(pl.multiple_of(i * CHUNK, CHUNK), CHUNK), :])
            xT[i] = xt
            ssp[i] = jnp.sum(xt * xt, axis=0, keepdims=True)

        loop((q + 1) * NCH // 4, tchunk, q * NCH // 4)

    def scatter(part, slots, ss, rs):
        def one(k):
            @pl.when(k != p)
            def _():
                rcopy(part.at[k], slots.at[p], ss.at[k], rs.at[p], ddev(k)).start()
        return one

    loop(NCH, scatter(ssp, ssr, sS, rS))

    def ad_of(zz):
        p2 = (NX * zz + x) // PER
        return p2, rcopy(AZ.at[zz], AX.at[x, p], sAD.at[zz], rAD.at[p], ddev(p2))

    def az_in(zz):
        return rcopy(AZ.at[zz], AZ.at[zz], sAZ.at[0], rAZ.at[zz], zdev(lax.rem(z + 1, NZ)))

    @pl.when(holder)
    def _():
        def step(i):
            zz = lax.rem(z + i, NZ)

            @pl.when(i > 0)
            def _():
                az_in(zz).wait_recv()

            p2, d = ad_of(zz)

            @pl.when(p2 != p)
            def _():
                d.start()

            @pl.when(p2 == p)
            def _():
                AX[x, p] = AZ[zz]

        loop(NZ, step)

    for d in loads[2:]:
        d.wait()
    ident_r = eye(RANK, BF16)

    def rchunk(i):
        rT[i] = contract_last(
            ident_r, rv[pl.ds(pl.multiple_of(i * CHUNK, CHUNK), CHUNK), :]
        ).astype(BF16)

    loop(NCH, rchunk)

    def gathered(part, slots, rs):
        def one(d):
            p2 = lax.rem(p + d, NP)
            rcopy(slots.at[p2], slots.at[p2], rs.at[p2], rs.at[p2], ddev(p2)).wait_recv()

        loop(NP, one, 1)
        slots[p] = part[kp]
        total = slots[0]
        for i in range(1, NP):
            total = total + slots[i]
        return total

    def spread_all(buf, ss, rs):
        def one(d):
            rcopy(buf.at[p], buf.at[p], ss.at[d], rs.at[p], ddev(lax.rem(p + d, NP))).start()
        loop(NP, one, 1)

    def spread_wait(buf, rs):
        def one(k):
            @pl.when(k != p)
            def _():
                rcopy(buf.at[k], buf.at[k], rs.at[k], rs.at[k], ddev(lax.rem(p + 1, NP))).wait_recv()
        loop(NCH, one)

    @pl.when(owner)
    def _():
        total = gathered(ssp, ssr, rS)
        rsv[p] = lax.rsqrt(total * (1.0 / WIDTH) + norm_eps)
        spread_all(rsv, sR, rR)

    def ax(d):
        return rcopy(AX.at[x], AX.at[x], sAX.at[d], rAX.at[x], xdev(lax.rem(x + d, NX)))

    @pl.when(active)
    def _():
        def one(k):
            @pl.when(k != p)
            def _():
                rcopy(AX.at[x, k], AX.at[x, k], rAD.at[k], rAD.at[k], ddev(lax.rem(p + 1, NP))).wait_recv()
        loop(TILES + 1, one)
        loop(NX, lambda d: ax(d).start(), 1)

    e48 = eye(ROLLS)

    def col(row):
        return jnp.sum(e48 * row, axis=1, keepdims=True)

    rew = rewv[...]
    grp = grpv[...].astype(F32)
    dst = dstv[...].astype(F32)
    ln = lenv[...].astype(F32)
    rew_c, len_c = col(rew), col(ln)
    same = (col(grp) == grp).astype(F32)
    members = jnp.sum(same, axis=0, keepdims=True)
    mean = jnp.sum(same * rew_c, axis=0, keepdims=True) / members
    var = jnp.sum(same * (rew_c - mean) ** 2, axis=0, keepdims=True) / members
    advantage = (rew - mean) / jnp.sqrt(jnp.maximum(var, 0.25))
    tokens = jnp.sum((col(dst) == dst).astype(F32) * len_c, axis=0, keepdims=True)
    inv = 1.0 / tokens
    slot = lax.broadcasted_iota(jnp.int32, (ROLLS, CHUNK), 1)
    roll = lax.broadcasted_iota(jnp.int32, (ROLLS, CHUNK), 0)
    pick = (roll == slot // LMAX + kp * (CHUNK // LMAX)).astype(F32)

    def expand(column):
        return jnp.sum(pick * column, axis=0, keepdims=True)

    adv_s = expand(col(advantage))
    inv_s = expand(col(inv))
    len_s = expand(len_c)
    place = lax.rem(lax.broadcasted_iota(jnp.int32, (1, CHUNK), 1), LMAX).astype(F32)
    live = place < len_s

    spread_wait(rsv, rR)

    def nchunk(i):
        xT[i] = xT[i] * rsv[i]

    loop(NCH, nchunk)

    for x2 in range(NX):
        @pl.when((x2 != x) & act(x2))
        def _(x2=x2):
            rcopy(AX.at[x2], AX.at[x2], rAX.at[x2], rAX.at[x2], xdev(lax.rem(x + 1, NX))).wait_recv()

    e96 = eye(BLOCK)
    for j in range(PER):
        xs = lax.rem(j + 3 * p, 4)
        for k in range(TILES):
            r0 = BLOCK * j + 16 * (k // 2)
            W[r0:r0 + 16, 128 * (k % 2):128 * (k % 2) + 128] = AX[xs, k]
        grow = AX[xs, TILES].astype(F32)[0:1, 0:BLOCK]
        gfull[BLOCK * j:BLOCK * j + BLOCK, :] = jnp.broadcast_to(
            jnp.sum(e96 * grow, axis=1, keepdims=True), (BLOCK, CHUNK)
        )

    send_q = scatter(qp, qr, sQ, rQ)

    def qchunk(i):
        h = jnp.dot(W[...], rT[i], preferred_element_type=F32)
        zb = (xT[i] * gfull[...]).astype(BF16)
        zT[i] = zb
        qp[i] = jnp.sum(zb.astype(F32) * h, axis=0, keepdims=True)
        send_q(i)

    loop(NCH, qchunk)

    @pl.when(owner)
    def _():
        shift = gathered(qp, qr, rQ)
        drift = driftv[:, pl.ds(pl.multiple_of(kp * CHUNK, CHUNK), CHUNK)]
        gap = gapv[:, pl.ds(pl.multiple_of(kp * CHUNK, CHUNK), CHUNK)]
        logratio = drift + shift
        ratio = jnp.exp(logratio)
        keep = jnp.where(
            adv_s >= 0,
            (drift <= jnp.float32(upper_log)).astype(F32),
            (drift >= jnp.float32(lower_log)).astype(F32),
        )
        dshift = inv_s * (-adv_s * ratio * keep + kl_coef * (1.0 - jnp.exp(gap - logratio)))
        wv[p] = jnp.where(live, dshift, 0.0)
        spread_all(wv, sW, rW)

    spread_wait(wv, rW)

    def dchunk(i):
        dT[i] = (rT[i].astype(F32) * wv[i]).astype(BF16)

    loop(NCH, dchunk)
    g = contract_last(zT[0], dT[0])
    for i in range(1, NCH):
        g = g + contract_last(zT[i], dT[i])
    for j in range(PER):
        for k in range(TILES):
            r0 = BLOCK * j + 16 * (k // 2)
            CXs[j, k] = g[r0:r0 + 16, 128 * (k % 2):128 * (k % 2) + 128].astype(BF16)

    def cx(j):
        xs = lax.rem(j + 3 * p, 4)
        return xs, rcopy(CXs.at[j], CX.at[x], sCX.at[j], rCX.at[x], xdev(xs))

    for j in range(PER):
        xs, d = cx(j)

        @pl.when(xs != x)
        def _(d=d):
            d.start()

        @pl.when(xs == x)
        def _(j=j):
            CX[x] = CXs[j]

    def cz(d):
        z2 = lax.rem(z + d, NZ)
        return rcopy(CZs.at[z2], CZ.at[z], sCZ.at[d], rCZ.at[z], zdev(z2))

    def cd(d):
        return rcopy(CD.at[p], CD.at[p], sCD.at[d], rCD.at[p], ddev(lax.rem(p + d, NP)))

    @pl.when(active)
    def _():
        def cx_in(d):
            x2 = lax.rem(x + d, NX)
            rcopy(CX.at[x2], CX.at[x2], rCX.at[x2], rCX.at[x2], xdev(x2)).wait_recv()

        loop(NX, cx_in, 1)
        total = CX[0].astype(F32)
        for i in range(1, NX):
            total = total + CX[i].astype(F32)
        Sf[...] = total
        CZs[...] = total.astype(BF16)
        loop(NZ, lambda d: cz(d).start(), 1)
        CZ[z] = jnp.zeros((16, 128), BF16)

        def cz_in(d):
            z2 = lax.rem(z + d, NZ)
            rcopy(CZ.at[z2], CZ.at[z2], rCZ.at[z2], rCZ.at[z2], zdev(z2)).wait_recv()

        loop(NZ, cz_in, 1)
        tile = Sf[z]
        for i in range(NZ):
            tile = tile + CZ[i].astype(F32)
        CD[p] = tile.astype(BF16)
        loop(NP, lambda d: cd(d).start(), 1)

    def cf(zz):
        p2 = (NX * zz + x) // PER
        return p2, rcopy(CD.at[p2], CF.at[z], sCF.at[zz], rCF.at[z], zdev(zz))

    def cfstep(zz):
        p2, d = cf(zz)

        @pl.when(p2 != p)
        def _():
            rcopy(CD.at[p2], CD.at[p2], rCD.at[p2], rCD.at[p2], ddev(lax.rem(p + 1, NP))).wait_recv()

        @pl.when(zz != z)
        def _():
            d.start()

        @pl.when(zz == z)
        def _():
            CF[z] = CD[p2]

    loop(NZ, cfstep)

    def cf_in(d):
        z2 = lax.rem(z + d, NZ)
        rcopy(CF.at[z2], CF.at[z2], rCF.at[z2], rCF.at[z2], zdev(z2)).wait_recv()

    loop(NZ, cf_in, 1)
    for k in range(TILES):
        r0, c0 = 16 * (k // 2), 128 * (k % 2)
        grad_o[r0:r0 + 16, c0:c0 + 128] = CF[k].astype(F32)
    gsum = jnp.sum(grad_o[...] * adv[...].astype(F32), axis=1, keepdims=True)
    ggain_o[...] = jnp.sum(e96 * gsum, axis=0, keepdims=True) / gainv[...].astype(F32)

    @pl.when(holder)
    def _():
        loop(NZ, lambda d: az(d).wait_send(), 1)

        def one(zz):
            p2, d = ad_of(zz)

            @pl.when(p2 != p)
            def _():
                d.wait_send()

        loop(NZ, one)

    @pl.when(active)
    def _():
        loop(NX, lambda d: ax(d).wait_send(), 1)
        loop(NZ, lambda d: cz(d).wait_send(), 1)
        loop(NP, lambda d: cd(d).wait_send(), 1)

    def scattered(part, slots, ss, rs):
        def one(k):
            @pl.when(k != p)
            def _():
                rcopy(part.at[k], slots.at[p], ss.at[k], rs.at[p], ddev(k)).wait_send()
        return one

    loop(NCH, scattered(ssp, ssr, sS, rS))
    loop(NCH, scattered(qp, qr, sQ, rQ))

    @pl.when(owner)
    def _():
        def one(d):
            p2 = lax.rem(p + d, NP)
            rcopy(rsv.at[p], rsv.at[p], sR.at[d], rR.at[p], ddev(p2)).wait_send()
            rcopy(wv.at[p], wv.at[p], sW.at[d], rW.at[p], ddev(p2)).wait_send()
        loop(NP, one, 1)

    for j in range(PER):
        xs, d = cx(j)

        @pl.when(xs != x)
        def _(d=d):
            d.wait_send()

    def cfout(d):
        cf(lax.rem(z + d, NZ))[1].wait_send()

    loop(NZ, cfout, 1)


def per_device(x_slots, gain, adapter, readout, drift, ref_gap, rewards, groups, lengths, dest):
    V = pltpu.VMEM
    D = pltpu.SemaphoreType.DMA
    any_spec = pl.BlockSpec(memory_space=pl.ANY)
    vmem_spec = pl.BlockSpec(memory_space=pltpu.VMEM)
    grad, ggain = pl.pallas_call(
        kernel,
        out_shape=(
            jax.ShapeDtypeStruct((BLOCK, RANK), F32),
            jax.ShapeDtypeStruct((1, BLOCK), F32),
        ),
        in_specs=[any_spec] * 10,
        out_specs=(vmem_spec, vmem_spec),
        scratch_shapes=[
            V((SLOTS, FEAT), BF16), V((SLOTS, RANK), BF16), V((BLOCK, RANK), BF16), V((1, BLOCK), BF16),
            V((1, SLOTS), F32), V((1, SLOTS), F32), V((1, ROLLS), F32),
            V((1, ROLLS), jnp.int32), V((1, ROLLS), jnp.int32), V((1, ROLLS), jnp.int32),
            V((NCH, FEAT, CHUNK), F32), V((NCH, RANK, CHUNK), BF16), V((NCH, FEAT, CHUNK), BF16),
            V((NCH, RANK, CHUNK), BF16), V((FEAT, RANK), BF16), V((FEAT, CHUNK), F32),
            V((NCH, 1, CHUNK), F32), V((NP, 1, CHUNK), F32), V((NCH, 1, CHUNK), F32),
            V((NCH, 1, CHUNK), F32), V((NP, 1, CHUNK), F32), V((NCH, 1, CHUNK), F32),
            V((NZ, 16, 128), BF16), V((NX, TILES + 1, 16, 128), BF16),
            V((PER, TILES, 16, 128), BF16), V((NX, TILES, 16, 128), BF16),
            V((TILES, 16, 128), F32), V((TILES, 16, 128), BF16), V((NZ, 16, 128), BF16),
            V((NP, 16, 128), BF16), V((NZ, 16, 128), BF16),
            D((9,)), D((4,)),
            D((NZ,)), D((NZ,)), D((NZ,)), D((NP,)), D((NX,)), D((NX,)),
            D((NP,)), D((NP,)), D((NP,)), D((NP,)), D((NP,)), D((NP,)), D((NP,)), D((NP,)),
            D((NX,)), D((NX,)), D((NZ,)), D((NZ,)), D((NP,)), D((NP,)), D((NZ,)), D((NZ,)),
        ],
        compiler_params=pltpu.CompilerParams(
            collective_id=0, has_side_effects=True, vmem_limit_bytes=48 * 1024 * 1024
        ),
    )(
        x_slots, gain.reshape(1, BLOCK), adapter, readout, drift, ref_gap, rewards, groups, lengths,
        dest,
    )
    return grad, ggain.reshape(BLOCK)


def solution(mesh):
    in_specs = (
        P("fsdp", None, "dp"),
        P("fsdp"),
        P("fsdp", None),
        P("fsdp", None, None),
        P("fsdp", None),
        P("fsdp", None),
        P("fsdp", None),
        P("fsdp", None),
        P("fsdp", None),
        P("fsdp", None),
    )
    out_specs = (P("fsdp", None), P("fsdp"))
    return jax.shard_map(
        per_device, mesh=mesh, in_specs=in_specs, out_specs=out_specs, check_vma=False
    )
```

time: 840 us -> 75.1 us (0.09)
  waiting for transfers between devices: 577 us -> 0 us
  blocking collectives: 176 us -> 0 us
  Pallas kernels: 0 us -> 67.8 us
  local copies, waits for them, and re-layouts: 36.4 us -> 5.51 us
  starting transfers between devices: 15 us -> 0 us
  between operations: 15.3 us -> 0.78 us
  other arithmetic: 12.9 us -> 0 us
    reduce_scatter x1 -> x0, waiting for transfers between devices: 453 us -> none  [per_device(): lax.psum_scatter(lax.dot_general(z_block, dlatent, (((0,), (0,)), ((), ()...]
    unnamed x1 -> x0, blocking collectives: 176 us -> none
    psum x1 -> x0, waiting for transfers between devices: 123 us -> none  [per_device(): grad_adapter = lax.psum(shard_sum, 'dp')]
    pallas_call x0 -> x1, Pallas kernels: none -> 67.8 us  [per_device(): pl.pallas_call(kernel, out_shape=(jax.ShapeDtypeStruct((BLOCK, RANK), F32...]
    gather x4 -> x0, local copies, waits for them, and re-layouts: 18.6 us -> none  [the longest x1 14.7 us: per_device(): local_rows[source_row.reshape(-1)]]
    all_to_all x1 -> x0, starting transfers between devices: 14.8 us -> none  [per_device(): lax.all_to_all(outgoing, 'dp', split_axis=0, concat_axis=1, tiled=True)]
    convert_element_type x2 -> x0, local copies, waits for them, and re-layouts: 10.5 us -> none  [per_device(): x_float = arrived.astype(jnp.float32)]
  transfers between devices with their start and end apart: 4 -> 0, of which waited for: 2 -> 0; matrix products, arithmetic and copies ran while one was open for 5% -> 0% of each run, Pallas kernels for 0% -> 0%
where the time goes in v1:
time: 75.1 us; the launch traced here: 74.1 us
  Pallas kernels  67.8 us (90%)
  local copies, waits for them, and re-layouts  5.51 us (7%)
  between operations  0.78 us (1%)
    pallas_call x1, Pallas kernels, per_device(): pl.pallas_call(kernel, out_shape=(jax.ShapeDtypeStruct((BLOCK, RANK), F32...  67.8 us
    unnamed x21, local copies, waits for them, and re-layouts  5.51 us

profile of v1, /device:TPU:1, one launch (start us, length us, event | category | flops | bytes accessed | tf_op | source)
XLA Modules:
  0.0 74.1 jit_solution(7721211800868098356)
XLA Ops:
  0.6 0.0 copy-start.1
  0.6 0.0 copy-start.2
  0.7 0.0 copy-start.3
  0.7 0.0 copy-start.4
  0.7 0.0 copy-start.5
  0.7 0.0 copy-start.6
  0.7 0.0 copy-start.7
  0.7 0.0 copy-start.8
  0.7 2.9 %copy.12.x_h = bf16[1,3072,288]{2,1,0:T(8,128)(2,1)S(1)} copy(bf16[1,3072,288]{1,2,0:T(8,128)(2,1)} %param.10) | data formatting | bytes 3538944 | tf_op args[0]
  3.6 0.0 copy-done.1
  3.6 0.0 copy-done.2
  3.7 0.0 copy-done.3
  3.7 0.0 copy-done.4
  3.7 0.0 copy-done.5
  3.7 0.0 copy-done.6
  3.7 0.0 copy-done.7
  3.7 0.0 copy-done.8
  3.7 0.0 copy-start
  3.7 1.4 %copy-done = bf16[1,3072,256]{2,1,0:T(8,128)(2,1)S(1)} copy-done((bf16[1,3072,256]{2,1,0:T(8,128)(2,1)S(1)}, bf16[1,3072,256]{2,1,0:T(8,128)(2,1)}, u32[]{:S(2)}) %copy-start) | copy-done | bytes 1572888
  5.1 67.8 %shard_map.113 = (f32[96,256]{1,0:T(8,128)S(1)}, f32[1,96]{1,0:T(1,128)S(1)}) custom-call(bf16[1,3072,288]{2,1,0:T(8,128)(2,1)S(1)} %copy.12.x_h, bf16[1,96]{1,0:T(2,128)(2,1)S(1)} %bitcast.2, bf16[96,256]{1,0:T(8,128)(2,1)S(1)} %copy-done.1, bf16[1,3072,256]{2,1,0:T(8,128)(2,1)S(1)} %copy-done, f32[1,3072]{1,0:T(1,128)S(1)} %copy-done.2, ...), custom_call_target="tpu_custom_call" | custom-call | tf_op jit(solution)/shard_map/pallas_call | solution.py:468
  73.0 0.6 copy.15
  73.6 0.5 copy.16
Async XLA Ops:
  0.6 3.0 %copy-start.1 = (bf16[96,256]{1,0:T(8,128)(2,1)S(1)}, bf16[96,256]{1,0:T(8,128)(2,1)}, u32[]{:S(2)}) copy-start(bf16[96,256]{1,0:T(8,128)(2,1)} %ad_h.1) | copy-start | bytes 147460
  0.6 3.0 %copy-start.2 = (f32[1,3072]{1,0:T(1,128)S(1)}, f32[1,3072]{1,0:T(1,128)}, u32[]{:S(2)}) copy-start(f32[1,3072]{1,0:T(1,128)} %drift_h.1) | copy-start | bytes 36868
  0.7 3.0 %copy-start.3 = (f32[1,3072]{1,0:T(1,128)S(1)}, f32[1,3072]{1,0:T(1,128)}, u32[]{:S(2)}) copy-start(f32[1,3072]{1,0:T(1,128)} %gap_h.1) | copy-start | bytes 36868
  0.7 3.0 %copy-start.4 = (bf16[96]{0:T(256)(128)(2,1)S(1)}, bf16[96]{0:T(256)(128)(2,1)}, u32[]{:S(2)}) copy-start(bf16[96]{0:T(256)(128)(2,1)} %param.11) | copy-start | bytes 580
  0.7 3.0 %copy-start.5 = (f32[1,48]{1,0:T(1,128)S(1)}, f32[1,48]{1,0:T(1,128)}, u32[]{:S(2)}) copy-start(f32[1,48]{1,0:T(1,128)} %rew_h.1) | copy-start | bytes 580
  0.7 3.0 %copy-start.6 = (s32[1,48]{1,0:T(1,128)S(1)}, s32[1,48]{1,0:T(1,128)}, u32[]{:S(2)}) copy-start(s32[1,48]{1,0:T(1,128)} %grp_h.1) | copy-start | bytes 580
  0.7 3.0 %copy-start.7 = (s32[1,48]{1,0:T(1,128)S(1)}, s32[1,48]{1,0:T(1,128)}, u32[]{:S(2)}) copy-start(s32[1,48]{1,0:T(1,128)} %len_h.1) | copy-start | bytes 580
  0.7 3.0 %copy-start.8 = (s32[1,48]{1,0:T(1,128)S(1)}, s32[1,48]{1,0:T(1,128)}, u32[]{:S(2)}) copy-start(s32[1,48]{1,0:T(1,128)} %dst_h.1) | copy-start | bytes 580
  3.7 1.4 %copy-start = (bf16[1,3072,256]{2,1,0:T(8,128)(2,1)S(1)}, bf16[1,3072,256]{2,1,0:T(8,128)(2,1)}, u32[]{:S(2)}) copy-start(bf16[1,3072,256]{2,1,0:T(8,128)(2,1)} %ro_h.1) | copy-start | bytes 4718596

commit v2 on v1

v2 whole, which is shorter than its diff:
```python
import math

import jax
import jax.numpy as jnp
from jax import lax
from jax.experimental import pallas as pl
from jax.experimental.pallas import tpu as pltpu
from jax.sharding import PartitionSpec as P

WIDTH = 4608
RANK = 256
SLOTS = 3072
LMAX = 64
ROLLS = 48
NP = 16
NZ = 12
NX = 4
FEAT = WIDTH // NP
BLOCK = WIDTH // (NZ * NX)
PER = FEAT // BLOCK
CHUNK = 256
NCH = SLOTS // CHUNK
TILES = 12
HALF = NCH // 2
GROUP = 4
FAR_Z = (6, 5, 7, 4, 8, 3, 9, 2, 10, 1, 11)
FAR_Y = (4, 3, 5, 2, 6, 1, 7)
FAR_P = (8, 7, 9, 6, 10, 5, 11, 4, 12, 3, 13, 2, 14, 1, 15)
kl_coef = 0.1
norm_eps = 1e-06
upper_log = math.log(1.2)
lower_log = math.log(0.8)
F32 = jnp.float32
BF16 = jnp.bfloat16
MESH = pl.DeviceIdType.MESH


def rcopy(src, dst, ssem, rsem, dev):
    return pltpu.make_async_remote_copy(
        src_ref=src, dst_ref=dst, send_sem=ssem, recv_sem=rsem, device_id=dev, device_id_type=MESH
    )


def loop(n, f, start=0):
    def step(i, carry):
        f(i)
        return carry

    lax.fori_loop(start, n, step, jnp.int32(0))


def eye(n, dtype=F32):
    r = lax.broadcasted_iota(jnp.int32, (n, n), 0)
    c = lax.broadcasted_iota(jnp.int32, (n, n), 1)
    return (r == c).astype(F32).astype(dtype)


def contract_last(a, b):
    return lax.dot_general(a, b, (((1,), (1,)), ((), ())), preferred_element_type=F32)


def kernel(
    x_h, gain_h, ad_h, ro_h, drift_h, gap_h, rew_h, grp_h, len_h, dst_h,
    grad_o, ggain_o,
    xv, rv, adv, gainv, driftv, gapv, rewv, grpv, lenv, dstv,
    rT, zT, dT, W, gfull,
    ssp, ssr, ssy, rsv, qp, qr, qy, wv, adv_s, inv_s, len_s,
    AZ, AX, CXs, CX, CZs, CM, CD,
    lsem, xsem,
    sAZ, rAZ, sAD, rAD, sAX, rAX,
    sS, rS, sQ, rQ,
    sCX, rCX, sCM, rCM, sCD, rCD,
):
    p = lax.axis_index("dp")
    c = lax.axis_index("fsdp")
    z = c // NX
    x = c % NX
    y = p // 2
    core = p % 2
    mine = core * HALF
    theirs = (1 - core) * HALF

    def zdev(z2):
        return (p, z2 * NX + x)

    def xdev(x2):
        return (p, z * NX + x2)

    def ddev(p2):
        return (p2, c)

    def act(x2):
        return lax.rem(x2 + p, 4) != 3

    sibling = (p + 1 - 2 * core, c)
    active = act(x)
    holder = p <= TILES
    owner = p < TILES

    small = [
        (ad_h, adv), (gain_h, gainv), (ro_h.at[0], rv), (drift_h, driftv), (gap_h, gapv), (rew_h, rewv),
        (grp_h, grpv), (len_h, lenv), (dst_h, dstv),
    ]
    loads = [pltpu.make_async_copy(s, d, lsem.at[i]) for i, (s, d) in enumerate(small)]
    xload = pltpu.make_async_copy(x_h, xv, xsem.at[0])
    loads[0].start()
    loads[1].start()
    xload.start()
    for d in loads[2:]:
        d.start()

    barrier = pltpu.get_barrier_semaphore()

    def greet(dev):
        pl.semaphore_signal(barrier, inc=1, device_id=dev, device_id_type=MESH)

    for d in FAR_Z:
        greet(zdev(lax.rem(z + d, NZ)))
    for d in FAR_Y:
        for k in range(2):
            greet(ddev(lax.rem(y + d, 8) * 2 + k))
    for d in (2, 1, 3):
        greet(xdev(lax.rem(x + d, NX)))
    greet(sibling)
    loads[0].wait()
    loads[1].wait()

    for k in range(TILES):
        @pl.when(p == k)
        def _(k=k):
            AZ[z] = adv[16 * (k // 2):16 * (k // 2) + 16, 128 * (k % 2):128 * (k % 2) + 128]

    @pl.when(p == TILES)
    def _():
        row = jnp.concatenate([gainv[...].astype(F32), jnp.ones((1, 128 - BLOCK), F32)], axis=1)
        AZ[z] = jnp.broadcast_to(row, (16, 128)).astype(BF16)

    xload.wait()
    for i in range(NCH):
        xt = xv[:, i * CHUNK:(i + 1) * CHUNK].astype(F32)
        ssp[i] = jnp.sum(xt * xt, axis=0, keepdims=True)

    pl.semaphore_wait(barrier, NZ + NX + NP - 3)

    def az(d):
        return rcopy(AZ.at[z], AZ.at[z], sAZ.at[d], rAZ.at[z], zdev(lax.rem(z + d, NZ)))

    @pl.when(holder)
    def _():
        for d in FAR_Z:
            az(d).start()

    def pair(src, dst, ss, rs, i):
        return rcopy(src, dst, ss.at[i], rs.at[i], sibling)

    def pair_half(part, got, ss, rs):
        return pair(part.at[pl.ds(theirs, HALF)], got, ss, rs, 8)

    def y_send(ys, ss, rs, d):
        return rcopy(ys.at[y], ys.at[y], ss.at[d], rs.at[y], ddev(lax.rem(y + d, 8) * 2 + core))

    def y_start(part, got, ys, ss, rs):
        pair_half(part, got, ss, rs).wait_recv()
        ys[y] = part[pl.ds(mine, HALF)] + got[...]
        for d in FAR_Y:
            y_send(ys, ss, rs, d).start()

    def y_sum(ys, ss, rs):
        for d in range(1, 8):
            y2 = lax.rem(y + d, 8)
            rcopy(ys.at[y2], ys.at[y2], ss.at[d], rs.at[y2], sibling).wait_recv()
        total = ys[0]
        for i in range(1, 8):
            total = total + ys[i]
        return total

    def pair_back(out, ss, rs):
        part = out.at[pl.ds(mine, HALF)]
        return pair(part, part, ss, rs, 9)

    def pair_back_in(out, ss, rs):
        part = out.at[pl.ds(theirs, HALF)]
        return pair(part, part, ss, rs, 9)

    pair_half(ssp, ssr, sS, rS).start()

    for d in loads[2:]:
        d.wait()
    ident = eye(RANK, BF16)
    for i in range(NCH):
        rT[i] = contract_last(ident, rv[i * CHUNK:(i + 1) * CHUNK, :]).astype(BF16)

    y_start(ssp, ssr, ssy, sS, rS)

    e48 = eye(ROLLS)

    def col(row):
        return jnp.sum(e48 * row, axis=1, keepdims=True)

    rew = rewv[...]
    grp = grpv[...].astype(F32)
    dst = dstv[...].astype(F32)
    ln = lenv[...].astype(F32)
    rew_c, len_c = col(rew), col(ln)
    same = (col(grp) == grp).astype(F32)
    members = jnp.sum(same, axis=0, keepdims=True)
    mean = jnp.sum(same * rew_c, axis=0, keepdims=True) / members
    var = jnp.sum(same * (rew_c - mean) ** 2, axis=0, keepdims=True) / members
    advantage = (rew - mean) / jnp.sqrt(jnp.maximum(var, 0.25))
    tokens = jnp.sum((col(dst) == dst).astype(F32) * len_c, axis=0, keepdims=True)
    adv_c, inv_c = col(advantage), col(1.0 / tokens)
    slot = lax.broadcasted_iota(jnp.int32, (ROLLS, CHUNK), 1)
    roll = lax.broadcasted_iota(jnp.int32, (ROLLS, CHUNK), 0)
    for i in range(HALF):
        pick = (roll == slot // LMAX + (mine + i) * (CHUNK // LMAX)).astype(F32)
        adv_s[i] = jnp.sum(pick * adv_c, axis=0, keepdims=True)
        inv_s[i] = jnp.sum(pick * inv_c, axis=0, keepdims=True)
        len_s[i] = jnp.sum(pick * len_c, axis=0, keepdims=True)

    def ad_of(zz):
        p2 = (NX * zz + x) // PER
        return p2, rcopy(AZ.at[zz], AX.at[x, p], sAD.at[zz], rAD.at[p], ddev(p2))

    @pl.when(holder)
    def _():
        for i in (0,) + FAR_Z[::-1]:
            zz = lax.rem(z + i, NZ)
            if i > 0:
                rcopy(AZ.at[zz], AZ.at[zz], sAZ.at[0], rAZ.at[zz], sibling).wait_recv()
            p2, d = ad_of(zz)

            @pl.when(p2 != p)
            def _(d=d):
                d.start()

            @pl.when(p2 == p)
            def _(zz=zz):
                AX[x, p] = AZ[zz]

    total = y_sum(ssy, sS, rS)
    rsv[pl.ds(mine, HALF)] = lax.rsqrt(total * (1.0 / WIDTH) + norm_eps)
    pair_back(rsv, sS, rS).start()

    def ax(k, d):
        return rcopy(AX.at[x, k], AX.at[x, k], sAX.at[d], rAX.at[x], xdev(lax.rem(x + d, NX)))

    @pl.when(active)
    def _():
        def one(i):
            m = i // 2
            dy = jnp.where(lax.rem(m, 2) == 1, (m + 1) // 2, 8 - m // 2)
            k = lax.rem(y + dy, 8) * 2 + lax.rem(i, 2)

            @pl.when(k <= TILES)
            def _():
                @pl.when(k != p)
                def _():
                    rcopy(AX.at[x, k], AX.at[x, k], rAD.at[k], rAD.at[k], sibling).wait_recv()
                for d in (2, 1, 3):
                    ax(k, d).start()
        loop(NP, one)

    pair_back_in(rsv, sS, rS).wait_recv()
    for x2 in range(NX):
        @pl.when((x2 != x) & act(x2))
        def _(x2=x2):
            rcopy(AX.at[x2], AX.at[x2], rAX.at[x2], rAX.at[x2], sibling).wait_recv()

    e96 = eye(BLOCK)
    for j in range(PER):
        xs = lax.rem(j + 3 * p, 4)
        for k in range(TILES):
            r0 = BLOCK * j + 16 * (k // 2)
            W[r0:r0 + 16, 128 * (k % 2):128 * (k % 2) + 128] = AX[xs, k]
        grow = AX[xs, TILES].astype(F32)[0:1, 0:BLOCK]
        gfull[BLOCK * j:BLOCK * j + BLOCK, :] = jnp.broadcast_to(
            jnp.sum(e96 * grow, axis=1, keepdims=True), (BLOCK, CHUNK)
        )

    def qchunk(i):
        at = pl.multiple_of(i * CHUNK, CHUNK)
        h = contract_last(W[...], rv[pl.ds(at, CHUNK), :])
        zb = (xv[:, pl.ds(at, CHUNK)].astype(F32) * rsv[i] * gfull[...]).astype(BF16)
        zT[i] = zb
        qp[i] = jnp.sum(zb.astype(F32) * h, axis=0, keepdims=True)

    for i in range(HALF):
        qchunk(theirs + i)
    pair_half(qp, qr, sQ, rQ).start()
    for i in range(HALF):
        qchunk(mine + i)
    y_start(qp, qr, qy, sQ, rQ)
    shift = y_sum(qy, sQ, rQ)
    drift = driftv[pl.ds(mine, HALF)]
    gap = gapv[pl.ds(mine, HALF)]
    adv_rows = adv_s[...]
    logratio = drift + shift
    ratio = jnp.exp(logratio)
    keep = jnp.where(
        adv_rows >= 0,
        (drift <= jnp.float32(upper_log)).astype(F32),
        (drift >= jnp.float32(lower_log)).astype(F32),
    )
    dshift = inv_s[...] * (-adv_rows * ratio * keep + kl_coef * (1.0 - jnp.exp(gap - logratio)))
    place = lax.rem(lax.broadcasted_iota(jnp.int32, (HALF, 1, CHUNK), 2), LMAX).astype(F32)
    wv[pl.ds(mine, HALF)] = jnp.where(place < len_s[...], dshift, 0.0)
    pair_back(wv, sQ, rQ).start()
    for i in range(HALF):
        dT[mine + i] = (rT[mine + i].astype(F32) * wv[mine + i]).astype(BF16)
    pair_back_in(wv, sQ, rQ).wait_recv()
    for i in range(HALF):
        dT[theirs + i] = (rT[theirs + i].astype(F32) * wv[theirs + i]).astype(BF16)

    g = contract_last(zT[0], dT[0])
    for i in range(1, NCH):
        g = g + contract_last(zT[i], dT[i])
    for j in range(PER):
        for k in range(TILES):
            r0 = BLOCK * j + 16 * (k // 2)
            CXs[j, k] = g[r0:r0 + 16, 128 * (k % 2):128 * (k % 2) + 128].astype(BF16)

    def cx(j, s):
        xs = lax.rem(j + 3 * p, 4)
        part = pl.ds(GROUP * s, GROUP)
        return xs, rcopy(CXs.at[j, part], CX.at[x, part], sCX.at[j, s], rCX.at[x, s], xdev(xs))

    for s in range(TILES // GROUP):
        for j in range(PER):
            xs, d = cx(j, s)

            @pl.when(xs != x)
            def _(d=d):
                d.start()

    for j in range(PER):
        @pl.when(lax.rem(j + 3 * p, 4) == x)
        def _(j=j):
            CX[x] = CXs[j]

    block = PER * p + jnp.minimum(lax.rem(x + p, 4), PER - 1)
    at_home = block // NX == z

    def cm(k):
        return rcopy(CZs.at[k], CM.at[z], sCM.at[k], rCM.at[z], (k, block))

    @pl.when(active)
    def _():
        for s in range(TILES // GROUP):
            part = pl.ds(GROUP * s, GROUP)
            for d in (1, 3, 2):
                x2 = lax.rem(x + d, NX)
                rcopy(CX.at[x2, part], CX.at[x2, part], rCX.at[x2, s], rCX.at[x2, s], sibling).wait_recv()
            total = CX[0, part].astype(F32)
            for i in range(1, NX):
                total = total + CX[i, part].astype(F32)
            CZs[part] = total.astype(BF16)
            for k in range(GROUP * s, GROUP * s + GROUP):
                @pl.when(jnp.logical_not(at_home & (p == k)))
                def _(k=k):
                    cm(k).start()

                @pl.when(at_home & (p == k))
                def _(k=k):
                    CM[z] = CZs[k]

    feeder = c // PER

    def cd(d):
        return rcopy(CD.at[p], CD.at[p], sCD.at[d], rCD.at[p], ddev(lax.rem(p + d, NP)))

    @pl.when(owner)
    def _():
        for d in (0,) + FAR_Z[::-1]:
            zz = lax.rem(z + d, NZ)

            def arrive(zz=zz):
                rcopy(CM.at[zz], CM.at[zz], rCM.at[zz], rCM.at[zz], sibling).wait_recv()

            if d == 0:
                pl.when(feeder != p)(arrive)
            else:
                arrive()
        tile = CM[0].astype(F32)
        for i in range(1, NZ):
            tile = tile + CM[i].astype(F32)
        CD[p] = tile.astype(BF16)
        for d in FAR_P:
            cd(d).start()

    for k in range(TILES):
        @pl.when(p != k)
        def _(k=k):
            rcopy(CD.at[k], CD.at[k], rCD.at[k], rCD.at[k], sibling).wait_recv()
    for k in range(TILES):
        r0, c0 = 16 * (k // 2), 128 * (k % 2)
        grad_o[r0:r0 + 16, c0:c0 + 128] = CD[k].astype(F32)
    gsum = jnp.sum(grad_o[...] * adv[...].astype(F32), axis=1, keepdims=True)
    ggain_o[...] = jnp.sum(e96 * gsum, axis=0, keepdims=True) / gainv[...].astype(F32)

    @pl.when(holder)
    def _():
        loop(NZ, lambda d: az(d).wait_send(), 1)

        def one(zz):
            p2, d = ad_of(zz)

            @pl.when(p2 != p)
            def _():
                d.wait_send()

        loop(NZ, one)

    @pl.when(active)
    def _():
        for d in range(1, NX):
            whole = AX.at[x]
            rcopy(whole, whole, sAX.at[d], rAX.at[x], xdev(lax.rem(x + d, NX))).wait_send()
        for k in range(TILES):
            @pl.when(jnp.logical_not(at_home & (p == k)))
            def _(k=k):
                cm(k).wait_send()

    for part, got, ys, out, ss, rs in ((ssp, ssr, ssy, rsv, sS, rS), (qp, qr, qy, wv, sQ, rQ)):
        pair_half(part, got, ss, rs).wait_send()
        for d in range(1, 8):
            y_send(ys, ss, rs, d).wait_send()
        pair_back(out, ss, rs).wait_send()

    for s in range(TILES // GROUP):
        for j in range(PER):
            xs, d = cx(j, s)

            @pl.when(xs != x)
            def _(d=d):
                d.wait_send()

    @pl.when(owner)
    def _():
        loop(NP, lambda d: cd(d).wait_send(), 1)


def per_device(x_slots, gain, adapter, readout, drift, ref_gap, rewards, groups, lengths, dest):
    V = pltpu.VMEM
    D = pltpu.SemaphoreType.DMA
    hbm_spec = pl.BlockSpec(memory_space=pltpu.HBM)
    vmem_spec = pl.BlockSpec(memory_space=pltpu.VMEM)
    chunks = V((NCH, 1, CHUNK), F32)
    half = V((HALF, 1, CHUNK), F32)
    along_y = V((8, HALF, 1, CHUNK), F32)
    grad, ggain = pl.pallas_call(
        kernel,
        out_shape=(
            jax.ShapeDtypeStruct((BLOCK, RANK), F32),
            jax.ShapeDtypeStruct((1, BLOCK), F32),
        ),
        in_specs=[hbm_spec] * 10,
        out_specs=(vmem_spec, vmem_spec),
        scratch_shapes=[
            V((FEAT, SLOTS), BF16), V((SLOTS, RANK), BF16), V((BLOCK, RANK), BF16), V((1, BLOCK), BF16),
            chunks, chunks, V((1, ROLLS), F32),
            V((1, ROLLS), jnp.int32), V((1, ROLLS), jnp.int32), V((1, ROLLS), jnp.int32),
            V((NCH, RANK, CHUNK), BF16), V((NCH, FEAT, CHUNK), BF16),
            V((NCH, RANK, CHUNK), BF16), V((FEAT, RANK), BF16), V((FEAT, CHUNK), F32),
            chunks, half, along_y, chunks, chunks, half, along_y, chunks, half, half, half,
            V((NZ, 16, 128), BF16), V((NX, TILES + 1, 16, 128), BF16),
            V((PER, TILES, 16, 128), BF16), V((NX, TILES, 16, 128), BF16),
            V((TILES, 16, 128), BF16), V((NZ, 16, 128), BF16), V((TILES, 16, 128), BF16),
            D((9,)), D((1,)),
            D((NZ,)), D((NZ,)), D((NZ,)), D((NP,)), D((NX,)), D((NX,)),
            D((10,)), D((10,)), D((10,)), D((10,)),
            D((PER, TILES // GROUP)), D((NX, TILES // GROUP)),
            D((TILES,)), D((NZ,)), D((NP,)), D((TILES,)),
        ],
        compiler_params=pltpu.CompilerParams(
            collective_id=0, has_side_effects=True, vmem_limit_bytes=60 * 1024 * 1024
        ),
    )(
        jnp.swapaxes(x_slots[0], 0, 1), gain.reshape(1, BLOCK), adapter, readout,
        drift.reshape(NCH, 1, CHUNK), ref_gap.reshape(NCH, 1, CHUNK), rewards, groups, lengths, dest,
    )
    return grad, ggain.reshape(BLOCK)


def solution(mesh):
    in_specs = (
        P("fsdp", None, "dp"),
        P("fsdp"),
        P("fsdp", None),
        P("fsdp", None, None),
        P("fsdp", None),
        P("fsdp", None),
        P("fsdp", None),
        P("fsdp", None),
        P("fsdp", None),
        P("fsdp", None),
    )
    out_specs = (P("fsdp", None), P("fsdp"))
    return jax.shard_map(
        per_device, mesh=mesh, in_specs=in_specs, out_specs=out_specs, check_vma=False
    )
```

time: 75.1 us -> 65.7 us (0.87); the launches traced: 74.1 us -> 65.5 us
  Pallas kernels: 67.8 us -> 62.1 us
  local copies, waits for them, and re-layouts: 5.51 us -> 2.73 us
    pallas_call x1, Pallas kernels: 67.8 us -> 62.1 us  [per_device(): pl.pallas_call(kernel, out_shape=(jax.ShapeDtypeStruct((BLOCK, RANK), F32...]
    unnamed x21 -> x2, local copies, waits for them, and re-layouts: 5.51 us -> 2.73 us
where the time goes in v2:
time: 65.7 us; the launch traced here: 65.5 us
  Pallas kernels  62.1 us (95%)
  local copies, waits for them, and re-layouts  2.73 us (4%)
    pallas_call x1, Pallas kernels, per_device(): pl.pallas_call(kernel, out_shape=(jax.ShapeDtypeStruct((BLOCK, RANK), F32...  62.1 us
    unnamed x2, local copies, waits for them, and re-layouts  2.73 us

profile of v2, /device:TPU:1, one launch (start us, length us, event | category | flops | bytes accessed | tf_op | source)
XLA Modules:
  0.0 65.5 jit_solution(4493634931303068067)
XLA Ops:
  0.6 62.1 %shard_map.113 = (f32[96,256]{1,0:T(8,128)}, f32[1,96]{1,0:T(1,128)}) custom-call(bf16[288,3072]{1,0:T(8,128)(2,1)} %bitcast.7, bf16[1,96]{1,0:T(2,128)(2,1)} %bitcast.10, bf16[96,256]{1,0:T(8,128)(2,1)} %ad_h.1, bf16[1,3072,256]{2,1,0:T(8,128)(2,1)} %ro_h.1, f32[12,1,256]{2,1,0:T(1,128)} %bitcast.8, f32[12,1,256]{2,1,0:T(1,128)} %bitcast.9, f32[1,48]{1,0:T(1,128)} %rew_h.1, ...), custom_call_target="tpu_custom_call" | custom-call | tf_op jit(solution)/shard_map/pallas_call | solution.py:450
  62.8 1.5 %copy.14 = f32[96,256]{1,0:T(8,128)} copy(f32[96,256]{1,0:T(8,128)} %get-tuple-element.8) | data formatting | bytes 196608
  64.3 1.2 %copy.15 = f32[96]{0:T(128)} copy(f32[96]{0:T(128)} %bitcast.11) | data formatting | bytes 768

commit v3 on v2

--- a/solution.py
+++ b/solution.py
@@ -24,6 +24,8 @@
 HALF = NCH // 2
 GROUP = 4
 FAR_Z = (6, 5, 7, 4, 8, 3, 9, 2, 10, 1, 11)
+PIECES = ((0, 48), (48, 32), (80, 32))
+NEAR_Z = (3, 9, 2, 10, 1, 11)
 FAR_Y = (4, 3, 5, 2, 6, 1, 7)
 FAR_P = (8, 7, 9, 6, 10, 5, 11, 4, 12, 3, 13, 2, 14, 1, 15)
 kl_coef = 0.1
@@ -61,13 +63,13 @@
 
 def kernel(
     x_h, gain_h, ad_h, ro_h, drift_h, gap_h, rew_h, grp_h, len_h, dst_h,
-    grad_o, ggain_o,
+    tiles_o,
     xv, rv, adv, gainv, driftv, gapv, rewv, grpv, lenv, dstv,
-    rT, zT, dT, W, gfull,
+    rT, zT, dT, W, gfull, gbuf,
     ssp, ssr, ssy, rsv, qp, qr, qy, wv, adv_s, inv_s, len_s,
-    AZ, AX, CXs, CX, CZs, CM, CD,
+    WX, CXs, CX, CZs, CM, CD,
     lsem, xsem,
-    sAZ, rAZ, sAD, rAD, sAX, rAX,
+    sAZ, rAZ, sAX, rAX,
     sS, rS, sQ, rQ,
     sCX, rCX, sCM, rCM, sCD, rCD,
 ):
@@ -94,18 +96,30 @@
 
     sibling = (p + 1 - 2 * core, c)
     active = act(x)
-    holder = p <= TILES
     owner = p < TILES
+    block = PER * p + jnp.minimum(lax.rem(x + p, 4), PER - 1)
+    away = lax.rem(z - block // NX + NZ, NZ)
 
     small = [
-        (ad_h, adv), (gain_h, gainv), (ro_h.at[0], rv), (drift_h, driftv), (gap_h, gapv), (rew_h, rewv),
-        (grp_h, grpv), (len_h, lenv), (dst_h, dstv),
+        (ad_h, adv), (gain_h, gainv),
+        (ro_h.at[0, pl.ds(theirs * CHUNK, SLOTS // 2)], rv.at[0:SLOTS // 2]),
+        (ro_h.at[0, pl.ds(mine * CHUNK, SLOTS // 2)], rv.at[SLOTS // 2:SLOTS]),
+        (rew_h, rewv), (grp_h, grpv), (len_h, lenv), (dst_h, dstv),
+        (drift_h.at[pl.ds(mine, HALF)], driftv), (gap_h.at[pl.ds(mine, HALF)], gapv),
     ]
     loads = [pltpu.make_async_copy(s, d, lsem.at[i]) for i, (s, d) in enumerate(small)]
-    xload = pltpu.make_async_copy(x_h, xv, xsem.at[0])
+    xloads = [
+        pltpu.make_async_copy(
+            x_h.at[:, pl.ds(pl.multiple_of(first * CHUNK, SLOTS // 2), SLOTS // 2)],
+            xv.at[:, i * (SLOTS // 2):(i + 1) * (SLOTS // 2)],
+            xsem.at[i],
+        )
+        for i, first in enumerate((theirs, mine))
+    ]
     loads[0].start()
     loads[1].start()
-    xload.start()
+    for d in xloads:
+        d.start()
     for d in loads[2:]:
         d.start()
 
@@ -114,54 +128,60 @@
     def greet(dev):
         pl.semaphore_signal(barrier, inc=1, device_id=dev, device_id_type=MESH)
 
-    for d in FAR_Z:
-        greet(zdev(lax.rem(z + d, NZ)))
     for d in FAR_Y:
         for k in range(2):
             greet(ddev(lax.rem(y + d, 8) * 2 + k))
+    for d in NEAR_Z:
+        greet(zdev(lax.rem(z + d, NZ)))
     for d in (2, 1, 3):
         greet(xdev(lax.rem(x + d, NX)))
     greet(sibling)
     loads[0].wait()
     loads[1].wait()
 
-    for k in range(TILES):
-        @pl.when(p == k)
-        def _(k=k):
-            AZ[z] = adv[16 * (k // 2):16 * (k // 2) + 16, 128 * (k % 2):128 * (k % 2) + 128]
-
-    @pl.when(p == TILES)
-    def _():
-        row = jnp.concatenate([gainv[...].astype(F32), jnp.ones((1, 128 - BLOCK), F32)], axis=1)
-        AZ[z] = jnp.broadcast_to(row, (16, 128)).astype(BF16)
-
-    xload.wait()
+    @pl.when(active & (away == 0))
+    def _():
+        row = jnp.concatenate([gainv[...].astype(F32), jnp.ones((1, RANK - BLOCK), F32)], axis=1)
+        WX[x, 0:16, :] = jnp.broadcast_to(row, (16, RANK)).astype(BF16)
+        WX[x, 16:16 + BLOCK, :] = adv[...]
+
+    pl.semaphore_wait(barrier, len(NEAR_Z) + NX + NP - 2)
+
+    def az(d, s):
+        part = WX.at[x, pl.ds(*PIECES[s])]
+        return rcopy(part, part, sAZ.at[d, s], rAZ.at[s], zdev(lax.rem(z + d, NZ)))
+
+    def az_all(dirs, s, act_on):
+        for d in dirs:
+            act_on(az(d, s))
+
+    ROUTES = ((0, NEAR_Z), (3, (3, 2, 1)), (9, (11, 10)))
+
+    @pl.when(active & (away == 0))
+    def _():
+        for s in range(len(PIECES)):
+            az_all((3, 9), s, lambda d: d.start())
+        for s in range(len(PIECES)):
+            az_all((2, 10, 1, 11), s, lambda d: d.start())
+
+    for d in xloads:
+        d.wait()
     for i in range(NCH):
         xt = xv[:, i * CHUNK:(i + 1) * CHUNK].astype(F32)
         ssp[i] = jnp.sum(xt * xt, axis=0, keepdims=True)
 
-    pl.semaphore_wait(barrier, NZ + NX + NP - 3)
-
-    def az(d):
-        return rcopy(AZ.at[z], AZ.at[z], sAZ.at[d], rAZ.at[z], zdev(lax.rem(z + d, NZ)))
-
-    @pl.when(holder)
-    def _():
-        for d in FAR_Z:
-            az(d).start()
-
     def pair(src, dst, ss, rs, i):
         return rcopy(src, dst, ss.at[i], rs.at[i], sibling)
 
     def pair_half(part, got, ss, rs):
-        return pair(part.at[pl.ds(theirs, HALF)], got, ss, rs, 8)
+        return pair(part.at[0:HALF], got, ss, rs, 8)
 
     def y_send(ys, ss, rs, d):
         return rcopy(ys.at[y], ys.at[y], ss.at[d], rs.at[y], ddev(lax.rem(y + d, 8) * 2 + core))
 
     def y_start(part, got, ys, ss, rs):
         pair_half(part, got, ss, rs).wait_recv()
-        ys[y] = part[pl.ds(mine, HALF)] + got[...]
+        ys[y] = part[HALF:NCH] + got[...]
         for d in FAR_Y:
             y_send(ys, ss, rs, d).start()
 
@@ -175,12 +195,7 @@
         return total
 
     def pair_back(out, ss, rs):
-        part = out.at[pl.ds(mine, HALF)]
-        return pair(part, part, ss, rs, 9)
-
-    def pair_back_in(out, ss, rs):
-        part = out.at[pl.ds(theirs, HALF)]
-        return pair(part, part, ss, rs, 9)
+        return pair(out.at[HALF:NCH], out.at[0:HALF], ss, rs, 9)
 
     pair_half(ssp, ssr, sS, rS).start()
 
@@ -217,82 +232,68 @@
         inv_s[i] = jnp.sum(pick * inv_c, axis=0, keepdims=True)
         len_s[i] = jnp.sum(pick * len_c, axis=0, keepdims=True)
 
-    def ad_of(zz):
-        p2 = (NX * zz + x) // PER
-        return p2, rcopy(AZ.at[zz], AX.at[x, p], sAD.at[zz], rAD.at[p], ddev(p2))
-
-    @pl.when(holder)
-    def _():
-        for i in (0,) + FAR_Z[::-1]:
-            zz = lax.rem(z + i, NZ)
-            if i > 0:
-                rcopy(AZ.at[zz], AZ.at[zz], sAZ.at[0], rAZ.at[zz], sibling).wait_recv()
-            p2, d = ad_of(zz)
-
-            @pl.when(p2 != p)
-            def _(d=d):
-                d.start()
-
-            @pl.when(p2 == p)
-            def _(zz=zz):
-                AX[x, p] = AZ[zz]
+    def ax(d, s):
+        part = WX.at[x, pl.ds(*PIECES[s])]
+        return rcopy(part, part, sAX.at[d, s], rAX.at[x, s], xdev(lax.rem(x + d, NX)))
+
+    @pl.when(active)
+    def _():
+        for s in range(len(PIECES)):
+            part = WX.at[x, pl.ds(*PIECES[s])]
+
+            @pl.when(away != 0)
+            def _(part=part, s=s):
+                rcopy(part, part, rAZ.at[s], rAZ.at[s], sibling).wait_recv()
+
+            for place, dirs in ROUTES[1:]:
+                @pl.when(away == place)
+                def _(dirs=dirs, s=s):
+                    az_all(dirs, s, lambda d: d.start())
+
+            for d in (2, 1, 3):
+                ax(d, s).start()
 
     total = y_sum(ssy, sS, rS)
-    rsv[pl.ds(mine, HALF)] = lax.rsqrt(total * (1.0 / WIDTH) + norm_eps)
+    rsv[HALF:NCH] = lax.rsqrt(total * (1.0 / WIDTH) + norm_eps)
     pair_back(rsv, sS, rS).start()
 
-    def ax(k, d):
-        return rcopy(AX.at[x, k], AX.at[x, k], sAX.at[d], rAX.at[x], xdev(lax.rem(x + d, NX)))
-
-    @pl.when(active)
-    def _():
-        def one(i):
-            m = i // 2
-            dy = jnp.where(lax.rem(m, 2) == 1, (m + 1) // 2, 8 - m // 2)
-            k = lax.rem(y + dy, 8) * 2 + lax.rem(i, 2)
-
-            @pl.when(k <= TILES)
-            def _():
-                @pl.when(k != p)
-                def _():
-                    rcopy(AX.at[x, k], AX.at[x, k], rAD.at[k], rAD.at[k], sibling).wait_recv()
-                for d in (2, 1, 3):
-                    ax(k, d).start()
-        loop(NP, one)
-
-    pair_back_in(rsv, sS, rS).wait_recv()
+    pair_back(rsv, sS, rS).wait_recv()
     for x2 in range(NX):
         @pl.when((x2 != x) & act(x2))
         def _(x2=x2):
-            rcopy(AX.at[x2], AX.at[x2], rAX.at[x2], rAX.at[x2], sibling).wait_recv()
+            for s, piece in enumerate(PIECES):
+                part = WX.at[x2, pl.ds(*piece)]
+                rcopy(part, part, rAX.at[x2, s], rAX.at[x2, s], sibling).wait_recv()
 
     e96 = eye(BLOCK)
     for j in range(PER):
         xs = lax.rem(j + 3 * p, 4)
-        for k in range(TILES):
-            r0 = BLOCK * j + 16 * (k // 2)
-            W[r0:r0 + 16, 128 * (k % 2):128 * (k % 2) + 128] = AX[xs, k]
-        grow = AX[xs, TILES].astype(F32)[0:1, 0:BLOCK]
+        W[BLOCK * j:BLOCK * j + BLOCK, :] = WX[xs, 16:16 + BLOCK, :]
+        grow = WX[xs, 0:16, :].astype(F32)[0:1, 0:BLOCK]
         gfull[BLOCK * j:BLOCK * j + BLOCK, :] = jnp.broadcast_to(
             jnp.sum(e96 * grow, axis=1, keepdims=True), (BLOCK, CHUNK)
         )
 
     def qchunk(i):
-        at = pl.multiple_of(i * CHUNK, CHUNK)
-        h = contract_last(W[...], rv[pl.ds(at, CHUNK), :])
-        zb = (xv[:, pl.ds(at, CHUNK)].astype(F32) * rsv[i] * gfull[...]).astype(BF16)
-        zT[i] = zb
-        qp[i] = jnp.sum(zb.astype(F32) * h, axis=0, keepdims=True)
+        h = contract_last(W[...], rv[i * CHUNK:(i + 1) * CHUNK, :])
+        xt = xv[:, i * CHUNK:(i + 1) * CHUNK].astype(F32)
+        qp[i] = jnp.sum(xt * (h * gfull[...]), axis=0, keepdims=True) * rsv[i]
+
+    def zchunk(i):
+        xt = xv[:, i * CHUNK:(i + 1) * CHUNK].astype(F32)
+        zT[i] = (xt * rsv[i] * gfull[...]).astype(BF16)
 
     for i in range(HALF):
-        qchunk(theirs + i)
+        qchunk(i)
     pair_half(qp, qr, sQ, rQ).start()
-    for i in range(HALF):
-        qchunk(mine + i)
+    for i in range(HALF, NCH):
+        qchunk(i)
     y_start(qp, qr, qy, sQ, rQ)
+    for i in range(NCH):
+        zchunk(i)
     shift = y_sum(qy, sQ, rQ)
-    drift = driftv[pl.ds(mine, HALF)]
-    gap = gapv[pl.ds(mine, HALF)]
+    drift = driftv[...]
+    gap = gapv[...]
     adv_rows = adv_s[...]
     logratio = drift + shift
     ratio = jnp.exp(logratio)
@@ -303,17 +304,20 @@
     )
     dshift = inv_s[...] * (-adv_rows * ratio * keep + kl_coef * (1.0 - jnp.exp(gap - logratio)))
     place = lax.rem(lax.broadcasted_iota(jnp.int32, (HALF, 1, CHUNK), 2), LMAX).astype(F32)
-    wv[pl.ds(mine, HALF)] = jnp.where(place < len_s[...], dshift, 0.0)
+    wv[HALF:NCH] = jnp.where(place < len_s[...], dshift, 0.0)
     pair_back(wv, sQ, rQ).start()
-    for i in range(HALF):
-        dT[mine + i] = (rT[mine + i].astype(F32) * wv[mine + i]).astype(BF16)
-    pair_back_in(wv, sQ, rQ).wait_recv()
-    for i in range(HALF):
-        dT[theirs + i] = (rT[theirs + i].astype(F32) * wv[theirs + i]).astype(BF16)
-
-    g = contract_last(zT[0], dT[0])
-    for i in range(1, NCH):
-        g = g + contract_last(zT[i], dT[i])
+
+    def gsum(chunks):
+        total = None
+        for i in chunks:
+            dT[i] = (rT[i].astype(F32) * wv[i]).astype(BF16)
+            term = contract_last(zT[i], dT[i])
+            total = term if total is None else total + term
+        return total
+
+    gbuf[...] = gsum(range(HALF, NCH))
+    pair_back(wv, sQ, rQ).wait_recv()
+    g = gsum(range(HALF)) + gbuf[...]
     for j in range(PER):
         for k in range(TILES):
             r0 = BLOCK * j + 16 * (k // 2)
@@ -337,7 +341,6 @@
         def _(j=j):
             CX[x] = CXs[j]
 
-    block = PER * p + jnp.minimum(lax.rem(x + p, 4), PER - 1)
     at_home = block // NX == z
 
     def cm(k):
@@ -391,30 +394,18 @@
         @pl.when(p != k)
         def _(k=k):
             rcopy(CD.at[k], CD.at[k], rCD.at[k], rCD.at[k], sibling).wait_recv()
-    for k in range(TILES):
-        r0, c0 = 16 * (k // 2), 128 * (k % 2)
-        grad_o[r0:r0 + 16, c0:c0 + 128] = CD[k].astype(F32)
-    gsum = jnp.sum(grad_o[...] * adv[...].astype(F32), axis=1, keepdims=True)
-    ggain_o[...] = jnp.sum(e96 * gsum, axis=0, keepdims=True) / gainv[...].astype(F32)
-
-    @pl.when(holder)
-    def _():
-        loop(NZ, lambda d: az(d).wait_send(), 1)
-
-        def one(zz):
-            p2, d = ad_of(zz)
-
-            @pl.when(p2 != p)
-            def _():
-                d.wait_send()
-
-        loop(NZ, one)
+    tiles_o[...] = CD[...]
 
     @pl.when(active)
     def _():
-        for d in range(1, NX):
-            whole = AX.at[x]
-            rcopy(whole, whole, sAX.at[d], rAX.at[x], xdev(lax.rem(x + d, NX))).wait_send()
+        for s in range(len(PIECES)):
+            for place, dirs in ROUTES:
+                @pl.when(away == place)
+                def _(dirs=dirs, s=s):
+                    az_all(dirs, s, lambda d: d.wait_send())
+
+            for d in (1, 2, 3):
+                ax(d, s).wait_send()
         for k in range(TILES):
             @pl.when(jnp.logical_not(at_home & (p == k)))
             def _(k=k):
@@ -437,6 +428,14 @@
     @pl.when(owner)
     def _():
         loop(NP, lambda d: cd(d).wait_send(), 1)
+
+
+def finish(tiles, ad, gain, grad_o, ggain_o):
+    for k in range(TILES):
+        r0, c0 = 16 * (k // 2), 128 * (k % 2)
+        grad_o[r0:r0 + 16, c0:c0 + 128] = tiles[k].astype(F32)
+    gsum = jnp.sum(grad_o[...] * ad[...].astype(F32), axis=1, keepdims=True)
+    ggain_o[...] = jnp.sum(eye(BLOCK) * gsum, axis=0, keepdims=True) / gain[...].astype(F32)
 
 
 def per_device(x_slots, gain, adapter, readout, drift, ref_gap, rewards, groups, lengths, dest):
@@ -447,26 +446,23 @@
     chunks = V((NCH, 1, CHUNK), F32)
     half = V((HALF, 1, CHUNK), F32)
     along_y = V((8, HALF, 1, CHUNK), F32)
-    grad, ggain = pl.pallas_call(
+    tiles = pl.pallas_call(
         kernel,
-        out_shape=(
-            jax.ShapeDtypeStruct((BLOCK, RANK), F32),
-            jax.ShapeDtypeStruct((1, BLOCK), F32),
-        ),
+        out_shape=jax.ShapeDtypeStruct((TILES, 16, 128), BF16),
         in_specs=[hbm_spec] * 10,
-        out_specs=(vmem_spec, vmem_spec),
+        out_specs=vmem_spec,
         scratch_shapes=[
             V((FEAT, SLOTS), BF16), V((SLOTS, RANK), BF16), V((BLOCK, RANK), BF16), V((1, BLOCK), BF16),
-            chunks, chunks, V((1, ROLLS), F32),
+            half, half, V((1, ROLLS), F32),
             V((1, ROLLS), jnp.int32), V((1, ROLLS), jnp.int32), V((1, ROLLS), jnp.int32),
             V((NCH, RANK, CHUNK), BF16), V((NCH, FEAT, CHUNK), BF16),
-            V((NCH, RANK, CHUNK), BF16), V((FEAT, RANK), BF16), V((FEAT, CHUNK), F32),
+            V((NCH, RANK, CHUNK), BF16), V((FEAT, RANK), BF16), V((FEAT, CHUNK), F32), V((FEAT, RANK), F32),
             chunks, half, along_y, chunks, chunks, half, along_y, chunks, half, half, half,
-            V((NZ, 16, 128), BF16), V((NX, TILES + 1, 16, 128), BF16),
+            V((NX, BLOCK + 16, RANK), BF16),
             V((PER, TILES, 16, 128), BF16), V((NX, TILES, 16, 128), BF16),
             V((TILES, 16, 128), BF16), V((NZ, 16, 128), BF16), V((TILES, 16, 128), BF16),
-            D((9,)), D((1,)),
-            D((NZ,)), D((NZ,)), D((NZ,)), D((NP,)), D((NX,)), D((NX,)),
+            D((10,)), D((2,)),
+            D((NZ, len(PIECES))), D((len(PIECES),)), D((NX, len(PIECES))), D((NX, len(PIECES))),
             D((10,)), D((10,)), D((10,)), D((10,)),
             D((PER, TILES // GROUP)), D((NX, TILES // GROUP)),
             D((TILES,)), D((NZ,)), D((NP,)), D((TILES,)),
@@ -478,6 +474,15 @@
         jnp.swapaxes(x_slots[0], 0, 1), gain.reshape(1, BLOCK), adapter, readout,
         drift.reshape(NCH, 1, CHUNK), ref_gap.reshape(NCH, 1, CHUNK), rewards, groups, lengths, dest,
     )
+    grad, ggain = pl.pallas_call(
+        finish,
+        out_shape=(
+            jax.ShapeDtypeStruct((BLOCK, RANK), F32),
+            jax.ShapeDtypeStruct((1, BLOCK), F32),
+        ),
+        in_specs=[vmem_spec] * 3,
+        out_specs=(vmem_spec, vmem_spec),
+    )(tiles, adapter, gain.reshape(1, BLOCK))
     return grad, ggain.reshape(BLOCK)
 
 

time: 65.7 us -> 61.3 us (0.933)
  local copies, waits for them, and re-layouts: 2.73 us -> 0 us
  Pallas kernels: 62.1 us -> 60.5 us
    unnamed x2 -> x0, local copies, waits for them, and re-layouts: 2.73 us -> none
    pallas_call x1 -> x2, Pallas kernels: 62.1 us -> 60.5 us  [the longest x1 59 us: per_device(): pl.pallas_call(kernel, out_shape=jax.ShapeDtypeStruct((TILES, 16, 128), B...]
where the time goes in v3:
time: 61.3 us; the launch traced here: 61.2 us
  Pallas kernels  60.5 us (99%)
  between operations  0.64 us (1%)
    pallas_call x1, Pallas kernels, per_device(): pl.pallas_call(kernel, out_shape=jax.ShapeDtypeStruct((TILES, 16, 128), B...  59 us
    pallas_call x1, Pallas kernels, per_device(): pl.pallas_call(finish, out_shape=(jax.ShapeDtypeStruct((BLOCK, RANK), F32...  1.48 us

profile of v3, /device:TPU:1, one launch (start us, length us, event | category | flops | bytes accessed | tf_op | source)
XLA Modules:
  0.0 61.2 jit_solution(530905277787385725)
XLA Ops:
  0.6 59.0 %shard_map.113.tiles = bf16[12,16,128]{2,1,0:T(8,128)(2,1)} custom-call(bf16[288,3072]{1,0:T(8,128)(2,1)} %bitcast.7, bf16[1,96]{1,0:T(2,128)(2,1)} %bitcast.10, bf16[96,256]{1,0:T(8,128)(2,1)} %ad.1, bf16[1,3072,256]{2,1,0:T(8,128)(2,1)} %ro_h.1, f32[12,1,256]{2,1,0:T(1,128)} %bitcast.8, f32[12,1,256]{2,1,0:T(1,128)} %bitcast.9, f32[1,48]{1,0:T(1,128)} %rew_h.1, ...), custom_call_target="tpu_custom_call" | custom-call | tf_op jit(solution)/shard_map/pallas_call | solution.py:449
  59.7 1.5 %shard_map.114 = (f32[96,256]{1,0:T(8,128)}, f32[1,96]{1,0:T(1,128)}) custom-call(bf16[12,16,128]{2,1,0:T(8,128)(2,1)} %shard_map.113.tiles, bf16[96,256]{1,0:T(8,128)(2,1)} %ad.1, bf16[1,96]{1,0:T(2,128)(2,1)} %bitcast.11), custom_call_target="tpu_custom_call" | custom-call | tf_op jit(solution)/shard_map/pallas_call | solution.py:477

commit v4 on v3

--- a/solution.py
+++ b/solution.py
@@ -67,11 +67,11 @@
     xv, rv, adv, gainv, driftv, gapv, rewv, grpv, lenv, dstv,
     rT, zT, dT, W, gfull, gbuf,
     ssp, ssr, ssy, rsv, qp, qr, qy, wv, adv_s, inv_s, len_s,
-    WX, CXs, CX, CZs, CM, CD,
+    WX, CXs, CX, CZs, CM, CR, CD,
     lsem, xsem,
     sAZ, rAZ, sAX, rAX,
     sS, rS, sQ, rQ,
-    sCX, rCX, sCM, rCM, sCD, rCD,
+    sCX, rCX, sCM, rCM, sCR, rCR, sCD, rCD,
 ):
     p = lax.axis_index("dp")
     c = lax.axis_index("fsdp")
@@ -277,11 +277,9 @@
     def qchunk(i):
         h = contract_last(W[...], rv[i * CHUNK:(i + 1) * CHUNK, :])
         xt = xv[:, i * CHUNK:(i + 1) * CHUNK].astype(F32)
-        qp[i] = jnp.sum(xt * (h * gfull[...]), axis=0, keepdims=True) * rsv[i]
-
-    def zchunk(i):
-        xt = xv[:, i * CHUNK:(i + 1) * CHUNK].astype(F32)
-        zT[i] = (xt * rsv[i] * gfull[...]).astype(BF16)
+        zb = (xt * rsv[i] * gfull[...]).astype(BF16)
+        zT[i] = zb
+        qp[i] = jnp.sum(zb.astype(F32) * h, axis=0, keepdims=True)
 
     for i in range(HALF):
         qchunk(i)
@@ -289,8 +287,6 @@
     for i in range(HALF, NCH):
         qchunk(i)
     y_start(qp, qr, qy, sQ, rQ)
-    for i in range(NCH):
-        zchunk(i)
     shift = y_sum(qy, sQ, rQ)
     drift = driftv[...]
     gap = gapv[...]
@@ -343,6 +339,12 @@
 
     at_home = block // NX == z
 
+    first_lines = block < NX
+
+    def cr(s):
+        part = pl.ds(GROUP * s, GROUP)
+        return rcopy(CZs.at[part], CR.at[z, part], sCR.at[s], rCR.at[z, s], (p, block))
+
     def cm(k):
         return rcopy(CZs.at[k], CM.at[z], sCM.at[k], rCM.at[z], (k, block))
 
@@ -357,21 +359,61 @@
             for i in range(1, NX):
                 total = total + CX[i, part].astype(F32)
             CZs[part] = total.astype(BF16)
-            for k in range(GROUP * s, GROUP * s + GROUP):
-                @pl.when(jnp.logical_not(at_home & (p == k)))
-                def _(k=k):
-                    cm(k).start()
-
-                @pl.when(at_home & (p == k))
-                def _(k=k):
-                    CM[z] = CZs[k]
+
+            @pl.when(jnp.logical_not(first_lines))
+            def _(s=s):
+                for k in range(GROUP * s, GROUP * s + GROUP):
+                    @pl.when(jnp.logical_not(at_home & (p == k)))
+                    def _(k=k):
+                        cm(k).start()
+
+                    @pl.when(at_home & (p == k))
+                    def _(k=k):
+                        CM[z] = CZs[k]
+
+            @pl.when(first_lines & jnp.logical_not(at_home))
+            def _(s=s):
+                cr(s).start()
+
+            @pl.when(first_lines & at_home)
+            def _(part=part):
+                CR[z, part] = CZs[part]
 
     feeder = c // PER
 
     def cd(d):
         return rcopy(CD.at[p], CD.at[p], sCD.at[d], rCD.at[p], ddev(lax.rem(p + d, NP)))
 
-    @pl.when(owner)
+    def spread_sib():
+        return rcopy(CD, CD, sCD.at[0], rCD.at[0], sibling)
+
+    def spread_y(d, k):
+        return rcopy(CD, CD, sCD.at[2 * d + k], rCD.at[0], ddev(lax.rem(y + d, 8) * 2 + k))
+
+    holds = feeder == p
+    in_first = c < NX
+
+    @pl.when(in_first & holds)
+    def _():
+        for s in range(TILES // GROUP):
+            part = pl.ds(GROUP * s, GROUP)
+            for d in FAR_Z[::-1]:
+                zz = lax.rem(z + d, NZ)
+                rcopy(CR.at[zz, part], CR.at[zz, part], rCR.at[zz, s], rCR.at[zz, s], sibling).wait_recv()
+            total = CR[0, part].astype(F32)
+            for i in range(1, NZ):
+                total = total + CR[i, part].astype(F32)
+            CD[part] = total.astype(BF16)
+        spread_sib().start()
+        for d in FAR_Y[::-1]:
+            for k in range(2):
+                spread_y(d, k).start()
+
+    @pl.when(in_first & jnp.logical_not(holds))
+    def _():
+        rcopy(CD, CD, rCD.at[0], rCD.at[0], sibling).wait_recv()
+
+    @pl.when(owner & jnp.logical_not(in_first))
     def _():
         for d in (0,) + FAR_Z[::-1]:
             zz = lax.rem(z + d, NZ)
@@ -391,7 +433,7 @@
             cd(d).start()
 
     for k in range(TILES):
-        @pl.when(p != k)
+        @pl.when((p != k) & jnp.logical_not(in_first))
         def _(k=k):
             rcopy(CD.at[k], CD.at[k], rCD.at[k], rCD.at[k], sibling).wait_recv()
     tiles_o[...] = CD[...]
@@ -407,9 +449,13 @@
             for d in (1, 2, 3):
                 ax(d, s).wait_send()
         for k in range(TILES):
-            @pl.when(jnp.logical_not(at_home & (p == k)))
+            @pl.when(jnp.logical_not(first_lines | (at_home & (p == k))))
             def _(k=k):
                 cm(k).wait_send()
+        for s in range(TILES // GROUP):
+            @pl.when(first_lines & jnp.logical_not(at_home))
+            def _(s=s):
+                cr(s).wait_send()
 
     for part, got, ys, out, ss, rs in ((ssp, ssr, ssy, rsv, sS, rS), (qp, qr, qy, wv, sQ, rQ)):
         pair_half(part, got, ss, rs).wait_send()
@@ -425,9 +471,16 @@
             def _(d=d):
                 d.wait_send()
 
-    @pl.when(owner)
+    @pl.when(owner & jnp.logical_not(in_first))
     def _():
         loop(NP, lambda d: cd(d).wait_send(), 1)
+
+    @pl.when(in_first & holds)
+    def _():
+        spread_sib().wait_send()
+        for d in FAR_Y:
+            for k in range(2):
+                spread_y(d, k).wait_send()
 
 
 def finish(tiles, ad, gain, grad_o, ggain_o):
@@ -460,12 +513,13 @@
             chunks, half, along_y, chunks, chunks, half, along_y, chunks, half, half, half,
             V((NX, BLOCK + 16, RANK), BF16),
             V((PER, TILES, 16, 128), BF16), V((NX, TILES, 16, 128), BF16),
-            V((TILES, 16, 128), BF16), V((NZ, 16, 128), BF16), V((TILES, 16, 128), BF16),
+            V((TILES, 16, 128), BF16), V((NZ, 16, 128), BF16), V((NZ, TILES, 16, 128), BF16),
+            V((TILES, 16, 128), BF16),
             D((10,)), D((2,)),
             D((NZ, len(PIECES))), D((len(PIECES),)), D((NX, len(PIECES))), D((NX, len(PIECES))),
             D((10,)), D((10,)), D((10,)), D((10,)),
             D((PER, TILES // GROUP)), D((NX, TILES // GROUP)),
-            D((TILES,)), D((NZ,)), D((NP,)), D((TILES,)),
+            D((TILES,)), D((NZ,)), D((TILES // GROUP,)), D((NZ, TILES // GROUP)), D((NP,)), D((TILES,)),
         ],
         compiler_params=pltpu.CompilerParams(
             collective_id=0, has_side_effects=True, vmem_limit_bytes=60 * 1024 * 1024

time: 61.3 us -> 59.4 us (0.969)
  the two profiles are of different devices: /device:TPU:1 before, /device:TPU:33 now
where the time goes in v4:
time: 59.4 us; the launch traced here: 59.2 us
  Pallas kernels  58.6 us (99%)
  between operations  0.64 us (1%)
    pallas_call x1, Pallas kernels, per_device(): pl.pallas_call(kernel, out_shape=jax.ShapeDtypeStruct((TILES, 16, 128), B...  57.1 us
    pallas_call x1, Pallas kernels, per_device(): pl.pallas_call(finish, out_shape=(jax.ShapeDtypeStruct((BLOCK, RANK), F32...  1.48 us

profile of v4, /device:TPU:33, one launch (start us, length us, event | category | flops | bytes accessed | tf_op | source)
XLA Modules:
  0.0 59.2 jit_solution(1294479522363930392)
XLA Ops:
  0.6 57.1 %shard_map.113.tiles = bf16[12,16,128]{2,1,0:T(8,128)(2,1)} custom-call(bf16[288,3072]{1,0:T(8,128)(2,1)} %bitcast.7, bf16[1,96]{1,0:T(2,128)(2,1)} %bitcast.10, bf16[96,256]{1,0:T(8,128)(2,1)} %ad.1, bf16[1,3072,256]{2,1,0:T(8,128)(2,1)} %ro_h.1, f32[12,1,256]{2,1,0:T(1,128)} %bitcast.8, f32[12,1,256]{2,1,0:T(1,128)} %bitcast.9, f32[1,48]{1,0:T(1,128)} %rew_h.1, ...), custom_call_target="tpu_custom_call" | custom-call | tf_op jit(solution)/shard_map/pallas_call | solution.py:502
  57.7 1.5 %shard_map.114 = (f32[96,256]{1,0:T(8,128)}, f32[1,96]{1,0:T(1,128)}) custom-call(bf16[12,16,128]{2,1,0:T(8,128)(2,1)} %shard_map.113.tiles, bf16[96,256]{1,0:T(8,128)(2,1)} %ad.1, bf16[1,96]{1,0:T(2,128)(2,1)} %bitcast.11), custom_call_target="tpu_custom_call" | custom-call | tf_op jit(solution)/shard_map/pallas_call | solution.py:531

commit v5 on v3

--- a/solution.py
+++ b/solution.py
@@ -23,6 +23,7 @@
 TILES = 12
 HALF = NCH // 2
 GROUP = 4
+FIRST = 12
 FAR_Z = (6, 5, 7, 4, 8, 3, 9, 2, 10, 1, 11)
 PIECES = ((0, 48), (48, 32), (80, 32))
 NEAR_Z = (3, 9, 2, 10, 1, 11)
@@ -67,11 +68,11 @@
     xv, rv, adv, gainv, driftv, gapv, rewv, grpv, lenv, dstv,
     rT, zT, dT, W, gfull, gbuf,
     ssp, ssr, ssy, rsv, qp, qr, qy, wv, adv_s, inv_s, len_s,
-    WX, CXs, CX, CZs, CM, CD,
+    WX, CXs, CX, CZs, CM, CN, CD,
     lsem, xsem,
     sAZ, rAZ, sAX, rAX,
     sS, rS, sQ, rQ,
-    sCX, rCX, sCM, rCM, sCD, rCD,
+    sCX, rCX, sCM, rCM, sCN, rCN, rCN2, sCD, rCD,
 ):
     p = lax.axis_index("dp")
     c = lax.axis_index("fsdp")
@@ -277,11 +278,9 @@
     def qchunk(i):
         h = contract_last(W[...], rv[i * CHUNK:(i + 1) * CHUNK, :])
         xt = xv[:, i * CHUNK:(i + 1) * CHUNK].astype(F32)
-        qp[i] = jnp.sum(xt * (h * gfull[...]), axis=0, keepdims=True) * rsv[i]
-
-    def zchunk(i):
-        xt = xv[:, i * CHUNK:(i + 1) * CHUNK].astype(F32)
-        zT[i] = (xt * rsv[i] * gfull[...]).astype(BF16)
+        zb = (xt * rsv[i] * gfull[...]).astype(BF16)
+        zT[i] = zb
+        qp[i] = jnp.sum(zb.astype(F32) * h, axis=0, keepdims=True)
 
     for i in range(HALF):
         qchunk(i)
@@ -289,8 +288,6 @@
     for i in range(HALF, NCH):
         qchunk(i)
     y_start(qp, qr, qy, sQ, rQ)
-    for i in range(NCH):
-        zchunk(i)
     shift = y_sum(qy, sQ, rQ)
     drift = driftv[...]
     gap = gapv[...]
@@ -343,6 +340,15 @@
 
     at_home = block // NX == z
 
+    first_lines = block < FIRST
+
+    def near_owner(plane, m):
+        return lax.rem(plane // 2 + 7 + m // 2, 8) * 2 + m % 2
+
+    def cn(m):
+        return rcopy(CZs.at[pl.ds(2 * m, 2)], CN.at[z], sCN.at[m], rCN.at[z], (near_owner(p, m), block))
+
+
     def cm(k):
         return rcopy(CZs.at[k], CM.at[z], sCM.at[k], rCM.at[z], (k, block))
 
@@ -357,21 +363,68 @@
             for i in range(1, NX):
                 total = total + CX[i, part].astype(F32)
             CZs[part] = total.astype(BF16)
-            for k in range(GROUP * s, GROUP * s + GROUP):
-                @pl.when(jnp.logical_not(at_home & (p == k)))
-                def _(k=k):
-                    cm(k).start()
-
-                @pl.when(at_home & (p == k))
-                def _(k=k):
-                    CM[z] = CZs[k]
+
+            @pl.when(first_lines)
+            def _(s=s):
+                for m in range(GROUP * s // 2, GROUP * s // 2 + GROUP // 2):
+                    @pl.when(jnp.logical_not(at_home & (p == near_owner(p, m))))
+                    def _(m=m):
+                        cn(m).start()
+
+                    @pl.when(at_home & (p == near_owner(p, m)))
+                    def _(m=m):
+                        CN[z] = CZs[2 * m:2 * m + 2]
+
+            @pl.when(block >= FIRST)
+            def _(s=s):
+                for k in range(GROUP * s, GROUP * s + GROUP):
+                    @pl.when(jnp.logical_not(at_home & (p == k)))
+                    def _(k=k):
+                        cm(k).start()
+
+                    @pl.when(at_home & (p == k))
+                    def _(k=k):
+                        CM[z] = CZs[k]
 
     feeder = c // PER
 
     def cd(d):
         return rcopy(CD.at[p], CD.at[p], sCD.at[d], rCD.at[p], ddev(lax.rem(p + d, NP)))
 
-    @pl.when(owner)
+    in_first = c < FIRST
+    others = c >= FIRST
+
+    def cdn(m, d):
+        part = CD.at[pl.ds(2 * m, 2)]
+        return rcopy(part, part, sCD.at[d], rCN2.at[m], ddev(lax.rem(p + d, NP)))
+
+    for m in range(6):
+        @pl.when(in_first & (p == near_owner(feeder, m)))
+        def _(m=m):
+            for d in (0,) + FAR_Z[::-1]:
+                zz = lax.rem(z + d, NZ)
+
+                def arrive(zz=zz):
+                    rcopy(CN.at[zz], CN.at[zz], rCN.at[zz], rCN.at[zz], sibling).wait_recv()
+
+                if d == 0:
+                    pl.when(feeder != p)(arrive)
+                else:
+                    arrive()
+            total = CN[0].astype(F32)
+            for i in range(1, NZ):
+                total = total + CN[i].astype(F32)
+            CD[2 * m:2 * m + 2] = total.astype(BF16)
+            for d in FAR_P[::-1]:
+                cdn(m, d).start()
+
+    for m in range(6):
+        @pl.when(in_first & (p != near_owner(feeder, m)))
+        def _(m=m):
+            part = CD.at[pl.ds(2 * m, 2)]
+            rcopy(part, part, rCN2.at[m], rCN2.at[m], sibling).wait_recv()
+
+    @pl.when(owner & others)
     def _():
         for d in (0,) + FAR_Z[::-1]:
             zz = lax.rem(z + d, NZ)
@@ -391,7 +444,7 @@
             cd(d).start()
 
     for k in range(TILES):
-        @pl.when(p != k)
+        @pl.when((p != k) & others)
         def _(k=k):
             rcopy(CD.at[k], CD.at[k], rCD.at[k], rCD.at[k], sibling).wait_recv()
     tiles_o[...] = CD[...]
@@ -407,9 +460,13 @@
             for d in (1, 2, 3):
                 ax(d, s).wait_send()
         for k in range(TILES):
-            @pl.when(jnp.logical_not(at_home & (p == k)))
+            @pl.when((block >= FIRST) & jnp.logical_not(at_home & (p == k)))
             def _(k=k):
                 cm(k).wait_send()
+        for m in range(6):
+            @pl.when(first_lines & jnp.logical_not(at_home & (p == near_owner(p, m))))
+            def _(m=m):
+                cn(m).wait_send()
 
     for part, got, ys, out, ss, rs in ((ssp, ssr, ssy, rsv, sS, rS), (qp, qr, qy, wv, sQ, rQ)):
         pair_half(part, got, ss, rs).wait_send()
@@ -425,9 +482,15 @@
             def _(d=d):
                 d.wait_send()
 
-    @pl.when(owner)
+    @pl.when(owner & others)
     def _():
         loop(NP, lambda d: cd(d).wait_send(), 1)
+
+    for m in range(6):
+        @pl.when(in_first & (p == near_owner(feeder, m)))
+        def _(m=m):
+            for d in FAR_P:
+                cdn(m, d).wait_send()
 
 
 def finish(tiles, ad, gain, grad_o, ggain_o):
@@ -460,12 +523,13 @@
             chunks, half, along_y, chunks, chunks, half, along_y, chunks, half, half, half,
             V((NX, BLOCK + 16, RANK), BF16),
             V((PER, TILES, 16, 128), BF16), V((NX, TILES, 16, 128), BF16),
-            V((TILES, 16, 128), BF16), V((NZ, 16, 128), BF16), V((TILES, 16, 128), BF16),
+            V((TILES, 16, 128), BF16), V((NZ, 16, 128), BF16),
+            V((NZ, 2, 16, 128), BF16), V((TILES, 16, 128), BF16),
             D((10,)), D((2,)),
             D((NZ, len(PIECES))), D((len(PIECES),)), D((NX, len(PIECES))), D((NX, len(PIECES))),
             D((10,)), D((10,)), D((10,)), D((10,)),
             D((PER, TILES // GROUP)), D((NX, TILES // GROUP)),
-            D((TILES,)), D((NZ,)), D((NP,)), D((TILES,)),
+            D((TILES,)), D((NZ,)), D((6,)), D((NZ,)), D((6,)), D((NP,)), D((TILES,)),
         ],
         compiler_params=pltpu.CompilerParams(
             collective_id=0, has_side_effects=True, vmem_limit_bytes=60 * 1024 * 1024

time: 61.3 us -> 58.5 us (0.954)
  Pallas kernels: 60.5 us -> 57.4 us
    pallas_call x1, Pallas kernels: 59 us -> 55.9 us  [per_device(): pl.pallas_call(kernel, out_shape=jax.ShapeDtypeStruct((TILES, 16, 128), B...]
where the time goes in v5:
time: 58.5 us; the launch traced here: 58 us
  Pallas kernels  57.4 us (98%)
  between operations  0.64 us (1%)
    pallas_call x1, Pallas kernels, per_device(): pl.pallas_call(kernel, out_shape=jax.ShapeDtypeStruct((TILES, 16, 128), B...  55.9 us
    pallas_call x1, Pallas kernels, per_device(): pl.pallas_call(finish, out_shape=(jax.ShapeDtypeStruct((BLOCK, RANK), F32...  1.48 us

profile of v5, /device:TPU:1, one launch (start us, length us, event | category | flops | bytes accessed | tf_op | source)
XLA Modules:
  0.0 58.0 jit_solution(17401231082194297024)
XLA Ops:
  0.6 55.9 %shard_map.113.tiles = bf16[12,16,128]{2,1,0:T(8,128)(2,1)} custom-call(bf16[288,3072]{1,0:T(8,128)(2,1)} %bitcast.7, bf16[1,96]{1,0:T(2,128)(2,1)} %bitcast.10, bf16[96,256]{1,0:T(8,128)(2,1)} %ad.1, bf16[1,3072,256]{2,1,0:T(8,128)(2,1)} %ro_h.1, f32[12,1,256]{2,1,0:T(1,128)} %bitcast.8, f32[12,1,256]{2,1,0:T(1,128)} %bitcast.9, f32[1,48]{1,0:T(1,128)} %rew_h.1, ...), custom_call_target="tpu_custom_call" | custom-call | tf_op jit(solution)/shard_map/pallas_call | solution.py:512
  56.5 1.5 %shard_map.114 = (f32[96,256]{1,0:T(8,128)}, f32[1,96]{1,0:T(1,128)}) custom-call(bf16[12,16,128]{2,1,0:T(8,128)(2,1)} %shard_map.113.tiles, bf16[96,256]{1,0:T(8,128)(2,1)} %ad.1, bf16[1,96]{1,0:T(2,128)(2,1)} %bitcast.11), custom_call_target="tpu_custom_call" | custom-call | tf_op jit(solution)/shard_map/pallas_call | solution.py:541

commit v6 on v5

--- a/solution.py
+++ b/solution.py
@@ -23,7 +23,7 @@
 TILES = 12
 HALF = NCH // 2
 GROUP = 4
-FIRST = 12
+FIRST = 18
 FAR_Z = (6, 5, 7, 4, 8, 3, 9, 2, 10, 1, 11)
 PIECES = ((0, 48), (48, 32), (80, 32))
 NEAR_Z = (3, 9, 2, 10, 1, 11)
@@ -278,9 +278,7 @@
     def qchunk(i):
         h = contract_last(W[...], rv[i * CHUNK:(i + 1) * CHUNK, :])
         xt = xv[:, i * CHUNK:(i + 1) * CHUNK].astype(F32)
-        zb = (xt * rsv[i] * gfull[...]).astype(BF16)
-        zT[i] = zb
-        qp[i] = jnp.sum(zb.astype(F32) * h, axis=0, keepdims=True)
+        qp[i] = jnp.sum(xt * (h * gfull[...]), axis=0, keepdims=True) * rsv[i]
 
     for i in range(HALF):
         qchunk(i)
@@ -288,6 +286,9 @@
     for i in range(HALF, NCH):
         qchunk(i)
     y_start(qp, qr, qy, sQ, rQ)
+    for i in range(NCH):
+        xt = xv[:, i * CHUNK:(i + 1) * CHUNK].astype(F32)
+        zT[i] = (xt * rsv[i] * gfull[...]).astype(BF16)
     shift = y_sum(qy, sQ, rQ)
     drift = driftv[...]
     gap = gapv[...]

time: 58.5 us -> 58.5 us (level)
  no operation moved by 1% of the time
where the time goes in v6:
time: 58.5 us; the launch traced here: 58 us
  Pallas kernels  57.4 us (98%)
  between operations  0.64 us (1%)
    pallas_call x1, Pallas kernels, per_device(): pl.pallas_call(kernel, out_shape=jax.ShapeDtypeStruct((TILES, 16, 128), B...  55.9 us
    pallas_call x1, Pallas kernels, per_device(): pl.pallas_call(finish, out_shape=(jax.ShapeDtypeStruct((BLOCK, RANK), F32...  1.48 us

profile of v6, /device:TPU:1, one launch (start us, length us, event | category | flops | bytes accessed | tf_op | source)
XLA Modules:
  0.0 58.0 jit_solution(4007542275456236726)
XLA Ops:
  0.6 55.9 %shard_map.113.tiles = bf16[12,16,128]{2,1,0:T(8,128)(2,1)} custom-call(bf16[288,3072]{1,0:T(8,128)(2,1)} %bitcast.7, bf16[1,96]{1,0:T(2,128)(2,1)} %bitcast.10, bf16[96,256]{1,0:T(8,128)(2,1)} %ad.1, bf16[1,3072,256]{2,1,0:T(8,128)(2,1)} %ro_h.1, f32[12,1,256]{2,1,0:T(1,128)} %bitcast.8, f32[12,1,256]{2,1,0:T(1,128)} %bitcast.9, f32[1,48]{1,0:T(1,128)} %rew_h.1, ...), custom_call_target="tpu_custom_call" | custom-call | tf_op jit(solution)/shard_map/pallas_call | solution.py:513
  56.5 1.5 %shard_map.114 = (f32[96,256]{1,0:T(8,128)}, f32[1,96]{1,0:T(1,128)}) custom-call(bf16[12,16,128]{2,1,0:T(8,128)(2,1)} %shard_map.113.tiles, bf16[96,256]{1,0:T(8,128)(2,1)} %ad.1, bf16[1,96]{1,0:T(2,128)(2,1)} %bitcast.11), custom_call_target="tpu_custom_call" | custom-call | tf_op jit(solution)/shard_map/pallas_call | solution.py:542
